TPU v7x, 256 devices: a whole 4x4x8 slice. The times are simulated.
256 devices in a mesh: seq: 64 (over z, y, core), hid: 4 (over x).
Axes of the slice: x: 4, y: 4, z: 8, core: 2. Of those that a mesh axis runs over, the one named last changes fastest.
Arguments:
- tokens: bfloat16 [65536, 768], P('seq', 'hid'), may hold values from -6 to 6
- first_gain: float32 [768], P('hid'), may hold values from 0.25 to 1.75
- first_shift: float32 [768], P('hid'), may hold values from -3 to 3
- inner_weight: bfloat16 [768, 3072], P(None, 'hid'), may hold values from -0.21875 to 0.21875
- inner_bias: float32 [3072], P('hid'), may hold values from -3 to 3
- outer_weight: bfloat16 [3072, 768], P('hid'), may hold values from -0.109375 to 0.109375
- outer_bias: float32 [768], P('hid'), may hold values from -3 to 3
- second_gain: float32 [768], P('hid'), may hold values from 0.25 to 1.75
- second_shift: float32 [768], P('hid'), may hold values from -3 to 3
Outputs:
- encoded: bfloat16 [65536, 768], P('seq', 'hid')
All inputs are finite; a program needn't handle non-finite values.
Results may differ from a plain program's by a relative error of at most 0.0051.
Values may be sent and summed in bfloat16 or wider, within the bound.
No kernel may reach another device: no remote copies, remote signals or barrier semaphores. Data moves between devices by JAX's collectives and lax.ppermute only.
A program may use at most 64 MiB of HBM per device.

v0:
```python
import math

import jax
import jax.numpy as jnp
import ml_dtypes
import numpy as np
from jax import lax
from jax.sharding import PartitionSpec as P

D = 768
HALF = D // 2
SEQ = 65536
R = 256
SEQ_DEVICES = 64
HID_DEVICES = 4
WIDTH = D // HID_DEVICES
EVERY = ("hid", "seq")
BF16 = ml_dtypes.bfloat16


def residues():
    place = np.arange(R)
    hid, seq = place // SEQ_DEVICES, place % SEQ_DEVICES
    chip = (seq >> 1) * HID_DEVICES + hid
    core = seq & 1
    return np.where(core == 0, chip, np.where(chip == 0, R // 2, R - chip)), chip, core


RESIDUE, CHIP, CORE = residues()
ROW = np.arange(R)
HIGH = HID_DEVICES * (ROW % SEQ_DEVICES) + ROW // SEQ_DEVICES


def cosine_sine(phase, period):
    angle = 2.0 * np.pi * (phase % period).astype(np.float64) / period
    return np.cos(angle), np.sin(angle)


def feature_table():
    rows = np.arange(D, dtype=np.int64)[:, None]
    columns = np.arange(HALF + 1, dtype=np.int64)[None, :]
    angle = np.float32(2.0 * math.pi / D) * (rows * columns % D).astype(np.float32)
    cosine = np.cos(angle.astype(np.float64)).astype(BF16)
    sine = (-np.sin(angle.astype(np.float64))).astype(BF16)
    sine[:, 0] = cosine[:, HALF]
    return np.concatenate([cosine[:, :HALF], sine[:, :HALF]], axis=1)


def make_tables():
    spread = (RESIDUE[:, None] == ROW[None, :]).astype(BF16)
    first_cos, first_sin = cosine_sine(RESIDUE[:, None] * HIGH[None, :], R)
    first = np.concatenate([first_cos, first_sin]).astype(BF16)
    base_cos, base_sin = cosine_sine(HIGH[:, None] * RESIDUE[None, :], R)
    base = np.stack([base_cos, base_sin]).astype(np.float32)
    own = cosine_sine(RESIDUE[:, None] * RESIDUE[None, :], SEQ)
    opposite = (R - RESIDUE) % R
    other = cosine_sine(opposite[:, None] * RESIDUE[None, :], SEQ)
    turn = np.stack([*own, *other], axis=1).astype(np.float32)
    lane = np.arange(HALF)
    mirror = (lane[:, None] == (HALF - lane[None, :]) % HALF).astype(BF16)
    return spread, first, base, turn, mirror


FEATURE = feature_table()
SPREAD, FIRST, BASE, TURN, MIRROR = make_tables()


def norm_rows(values, gain, shift):
    mean = jnp.mean(values, axis=1, keepdims=True)
    spread = jnp.mean(values * values, axis=1, keepdims=True) - mean * mean
    return (values - mean) * lax.rsqrt(spread + 1e-05) * gain + shift


def dot(left, right):
    return jnp.dot(left, right, preferred_element_type=jnp.float32)


def pair_index(seq, hid):
    return seq * HID_DEVICES + hid % HID_DEVICES


def ring(value, sign):
    pairs = []
    for seq in range(SEQ_DEVICES):
        step = -sign if seq & 1 else sign
        for hid in range(HID_DEVICES):
            pairs.append((pair_index(seq, hid), pair_index(seq, hid + step)))
    return lax.ppermute(value, ("seq", "hid"), pairs)


def swap_cores(value):
    return lax.ppermute(value, "seq", [(seq, seq ^ 1) for seq in range(SEQ_DEVICES)])


def swap_mirrored(value):
    pairs = []
    for seq in range(SEQ_DEVICES):
        for hid in range(HID_DEVICES):
            alone = seq < 2 and hid == 0
            pairs.append((pair_index(seq, hid), pair_index(seq if alone else seq ^ 1, hid)))
    return lax.ppermute(value, ("seq", "hid"), pairs)


def shift_hid(value, step):
    pairs = [(hid, (hid + step) % HID_DEVICES) for hid in range(HID_DEVICES)]
    return lax.ppermute(value, "hid", pairs)


def shards(
    tokens,
    first_gain,
    first_shift,
    inner_weight,
    inner_bias,
    outer_weight,
    outer_bias,
    second_gain,
    second_shift,
):
    bf16 = jnp.bfloat16
    f32 = jnp.float32
    seq = lax.axis_index("seq")
    hid = lax.axis_index("hid")
    core = seq & 1
    place = hid * SEQ_DEVICES + seq
    alone = place < 2

    hidden = inner_weight.shape[1]
    part = hidden // 2
    inner_half = lax.dynamic_slice_in_dim(inner_weight, core * part, part, 1)
    outer_half = lax.dynamic_slice_in_dim(outer_weight, core * part, part, 0)
    payload = jnp.concatenate([inner_half, outer_half[:, :HALF], outer_half[:, HALF:]], axis=0)
    ring_one = ring(payload, 1)
    ring_three = ring(payload, -1)
    ring_two = ring(ring_one, 1)
    others = [ring_one, ring_two, ring_three]
    others = others + [swap_cores(each) for each in others]
    small = jnp.concatenate(
        [
            first_gain[None],
            first_shift[None],
            outer_bias[None],
            second_gain[None],
            second_shift[None],
            inner_bias.reshape(HID_DEVICES, WIDTH),
        ]
    )
    around = [small, shift_hid(small, -1), shift_hid(small, 2), shift_hid(small, 1)]
    around = jnp.stack(around + around)
    vectors = lax.dynamic_slice_in_dim(around, (HID_DEVICES - hid) % HID_DEVICES, HID_DEVICES, 0)
    rows = jnp.transpose(vectors[:, :5], (1, 0, 2)).reshape(5, 1, D)
    biases = vectors[:, 5:].reshape(HID_DEVICES * 2, part)
    sign = 1 - 2 * core

    def bias_of(shard, half):
        index = (shard + HID_DEVICES) % HID_DEVICES * 2 + half
        return lax.dynamic_slice_in_dim(biases, index, 1, 0)

    other_biases = [
        bias_of(hid - sign, core),
        bias_of(hid + 2, core),
        bias_of(hid + sign, core),
        bias_of(hid + sign, 1 - core),
        bias_of(hid + 2, 1 - core),
        bias_of(hid - sign, 1 - core),
    ]

    blocks = tokens.reshape(HID_DEVICES, R, WIDTH)
    sent = jnp.einsum("dm,amc->dac", jnp.asarray(SPREAD), blocks, preferred_element_type=f32)
    sent = sent.astype(bf16).reshape(R, D)
    taken = lax.all_to_all(sent, EVERY, 0, 0, tiled=True)
    local = taken.reshape(HID_DEVICES, SEQ_DEVICES, HID_DEVICES, WIDTH)
    local = jnp.transpose(local, (2, 1, 0, 3)).reshape(R, D)

    features = dot(local, jnp.asarray(FEATURE)).astype(bf16)
    turned = dot(jnp.asarray(FIRST), features)
    cos_real, cos_imag = turned[:R, :HALF], turned[:R, HALF:]
    sin_real, sin_imag = turned[R:, :HALF], turned[R:, HALF:]
    lane = lax.broadcasted_iota(jnp.int32, (R, HALF), 1)
    row_core = jnp.asarray(CORE.astype(np.int32))[:, None]
    row_alone = jnp.asarray((CHIP == 0))[:, None]
    edge = lane == 0
    late = jnp.logical_and(row_core == 1, jnp.logical_not(row_alone))
    edge_real = jnp.where(late, cos_imag, cos_real)
    edge_imag = jnp.where(row_alone, cos_imag, -jnp.where(late, sin_imag, sin_real))
    spectrum_real = jnp.where(edge, edge_real, cos_real + sin_imag)
    spectrum_imag = jnp.where(edge, edge_imag, cos_imag - sin_real)
    sent = jnp.concatenate([spectrum_real, spectrum_imag], axis=1).astype(bf16)
    taken = lax.all_to_all(sent, EVERY, 0, 0, tiled=True)

    turn = lax.dynamic_slice_in_dim(jnp.asarray(TURN), place, 1, 0)[0]
    base_cos, base_sin = jnp.asarray(BASE[0]), jnp.asarray(BASE[1])
    own_cos = base_cos * turn[0] - base_sin * turn[1]
    own_sin = base_sin * turn[0] + base_cos * turn[1]
    other_cos = base_cos * turn[2] - base_sin * turn[3]
    other_sin = base_sin * turn[2] + base_cos * turn[3]
    real, imag = taken[:, :HALF], taken[:, HALF:]
    single = jnp.logical_and(edge, alone)
    zero = jnp.zeros((), bf16)
    imag_cut = jnp.where(single, zero, imag)
    real_cut = jnp.where(single, imag, real)
    own = dot(own_cos.astype(bf16), real) + dot(own_sin.astype(bf16), imag_cut)
    opposite = dot(other_cos.astype(bf16), real_cut) - dot(other_sin.astype(bf16), imag_cut)
    scale = 1.0 / math.sqrt(SEQ * D)
    received = swap_mirrored((opposite * scale).astype(bf16))
    own = own * scale
    crossed = jnp.logical_and(edge, jnp.logical_and(core == 1, jnp.logical_not(alone)))
    low = jnp.where(crossed, received.astype(f32), own)
    high = jnp.where(crossed, own, received.astype(f32)).astype(bf16)
    mixed = jnp.concatenate([low, dot(high, jnp.asarray(MIRROR))], axis=1)

    first_sum = local.astype(f32) + mixed
    normed = norm_rows(first_sum, rows[0], rows[1]).astype(bf16)

    inner = dot(normed, inner_weight) + inner_bias
    active = jax.nn.gelu(inner, approximate=True).astype(bf16)
    outer = dot(active, outer_weight)
    for each, bias in zip(others, other_biases):
        inner = dot(normed, each[:D]) + bias
        active = jax.nn.gelu(inner, approximate=True).astype(bf16)
        outer = outer + jnp.concatenate(
            [dot(active, each[D : D + part]), dot(active, each[D + part :])], axis=1
        )
    second_sum = normed.astype(f32) + outer + rows[2]
    finished = norm_rows(second_sum, rows[3], rows[4]).astype(bf16)

    sent = finished.reshape(HID_DEVICES, SEQ_DEVICES, HID_DEVICES, WIDTH)
    sent = jnp.transpose(sent, (2, 1, 0, 3)).reshape(R, D)
    taken = lax.all_to_all(sent, EVERY, 0, 0, tiled=True)
    ordered = jnp.einsum(
        "dm,dac->amc",
        jnp.asarray(SPREAD),
        taken.reshape(R, HID_DEVICES, WIDTH),
        preferred_element_type=f32,
    )
    return ordered.astype(bf16).reshape(tokens.shape)


def solution(mesh):
    return jax.shard_map(
        shards,
        mesh=mesh,
        in_specs=(
            P("seq", "hid"),
            P("hid"),
            P("hid"),
            P(None, "hid"),
            P("hid"),
            P("hid", None),
            P("hid"),
            P("hid"),
            P("hid"),
        ),
        out_specs=P("seq", "hid"),
        check_vma=False,
    )
```

profile of v0, /device:TPU:1, one launch (start us, length us, event | category | flops | bytes accessed | tf_op | source)
XLA Modules:
  0.0 157.8 jit_solution(13615064452904164865)
XLA Ops:
  0.0 0.9 reshape.152
  0.9 0.8 concatenate.49
  1.8 3.4 %collective-permute-start.1 = (f32[9,192]{1,0:T(8,128)S(1)}, f32[9,192]{1,0:T(8,128)S(1)}, u32[]{:S(2)}, u32[]{:S(2)}) collective-permute-start(f32[9,192]{1,0:T(8,128)S(1)} %concatenate.49), channel_id=1, source_target_pairs={{0,3},{1,0},{2,1},{3,2},{4,7},{5,4},{6,5},{7,6},{8,11},{9,8},{10,9... | collective-permute-start | bytes 20744 | tf_op jit(solution)/shard_map/ppermute | solution.py:106
  6.5 1.1 pad_maximum_fusion
  7.6 2.1 %collective-permute-start.4 = (bf16[1536,384]{1,0:T(8,128)(2,1)}, bf16[1536,384]{1,0:T(8,128)(2,1)}, u32[]{:S(2)}, u32[]{:S(2)}) collective-permute-start(bf16[1536,384]{1,0:T(8,128)(2,1)} %pad_maximum_fusion), channel_id=1, source_target_pairs={{0,1},{1,2},{2,3},{3,0},{4,7},{5,4},{6,5},{7,6},{8,9},{9,10},{10,1... | collective-permute-start | bytes 3538952 | tf_op jit(solution)/shard_map/ppermute | solution.py:88
  10.6 1.0 reduce.25
  11.8 0.8 reshape.172
  12.6 15.0 %all-to-all-start = ((bf16[256,2,384]{2,1,0:T(2,128)(2,1)}), bf16[256,2,384]{2,1,0:T(2,128)(2,1)S(1)}, u32[]{:S(2)}, u32[]{:S(2)}) async-start(bf16[256,2,384]{2,1,0:T(2,128)(2,1)} %reshape.172), calls=%async_computation | async-start | bytes 786432 | tf_op jit(solution)/shard_map/all_to_all | solution.py:171
  28.7 1.4 constant_dynamic-slice_fusion.3
  31.4 14.4 %all-to-all-done = bf16[256,2,384]{2,1,0:T(2,128)(2,1)S(1)} async-done(((bf16[256,2,384]{2,1,0:T(2,128)(2,1)}), bf16[256,2,384]{2,1,0:T(2,128)(2,1)S(1)}, u32[]{:S(2)}, u32[]{:S(2)}) %all-to-all-start) | async-done | bytes 393248 | tf_op jit(solution)/shard_map/all_to_all | solution.py:171
  46.1 2.4 %reduce.2 = bf16[256,768]{1,0:T(8,128)(2,1)S(1)} reduce(bf16[256,1,768]{2,1,0:T(2,128)(2,1)S(1)} %reshape.173, bf16[]{:T(256)} %constant.116), dimensions={1}, to_apply=%all_to_all.19.reduce_sub_computation | reduce | bytes 786434 | tf_op jit(solution)/shard_map/all_to_all | solution.py:171
  49.4 1.2 reshape.151
  50.6 2.2 %fusion = f32[512,768]{1,0:T(8,128)S(1)} fusion(bf16[512,256]{1,0:T(8,128)(2,1)S(1)} %copy-done.9, bf16[256,768]{1,0:T(8,128)(2,1)} %reshape.151, bf16[768,768]{1,0:T(8,128)(2,1)} %constant.104.clone), kind=kOutput, calls=%fused_computation.3 | convolution fusion | flops 503513088 | bytes 3407872 | tf_op jit(solution)/shard_map/dot_general | solution.py:75
  52.8 0.9 fusion.130
  53.7 1.0 reduce.26
  54.7 0.8 reshape.174
  55.5 10.2 %all-to-all-start.1 = ((bf16[256,2,384]{2,1,0:T(2,128)(2,1)}), bf16[256,2,384]{2,1,0:T(2,128)(2,1)S(1)}, u32[]{:S(2)}, u32[]{:S(2)}) async-start(bf16[256,2,384]{2,1,0:T(2,128)(2,1)} %reshape.174), calls=%async_computation.1 | async-start | bytes 786432 | tf_op jit(solution)/shard_map/all_to_all | solution.py:189
  67.6 2.7 %collective-permute-start.5 = (bf16[1536,384]{1,0:T(8,128)(2,1)}, bf16[1536,384]{1,0:T(8,128)(2,1)}, u32[]{:S(2)}, u32[]{:S(2)}) collective-permute-start(bf16[1536,384]{1,0:T(8,128)(2,1)} %collective-permute-done.4), channel_id=1, source_target_pairs={{0,1},{1,2},{2,3},{3,0},{4,7},{5,4},{6,5},{7,6},{8,9},{9,10},{10,1... | collective-permute-start | bytes 3538952 | tf_op jit(solution)/shard_map/ppermute | solution.py:88
  70.8 13.2 %all-to-all-done.1 = bf16[256,2,384]{2,1,0:T(2,128)(2,1)S(1)} async-done(((bf16[256,2,384]{2,1,0:T(2,128)(2,1)}), bf16[256,2,384]{2,1,0:T(2,128)(2,1)S(1)}, u32[]{:S(2)}, u32[]{:S(2)}) %all-to-all-start.1) | async-done | bytes 393248 | tf_op jit(solution)/shard_map/all_to_all | solution.py:189
  84.9 0.7 collective-permute-start
  87.1 1.0 pad_maximum_fusion.1
  88.1 1.9 %concatenate.48 = f32[4,64,4,192]{3,2,1,0:T(4,128)S(1)} reshape(f32[256,768]{1,0:T(8,128)} %pad_maximum_fusion.1) | data formatting | bytes 1572864 | tf_op jit(solution)/shard_map/concatenate | solution.py:210
  90.0 1.2 fusion.27
  91.5 1.2 add_convert_fusion.1
  92.7 1.6 %fusion.38 = bf16[256,384]{1,0:T(8,128)(2,1)S(1)} fusion(bf16[256,768]{1,0:T(8,128)(2,1)S(1)} %add_convert_fusion.1, bf16[1536,384]{1,0:T(8,128)(2,1)} %collective-permute-done.4, f32[384]{0:T(512)S(1)} %copy-done.28), kind=kOutput, calls=%fused_computation.65 | convolution fusion | flops 151977984 | bytes 1181184 | tf_op jit(solution)/shard_map/dot_general | solution.py:75
  94.4 1.2 fusion.126
  95.6 1.2 fusion.128
  96.9 1.5 fusion.62
  98.4 1.2 fusion.120
  99.7 1.2 fusion.118
  101.2 1.5 fusion.50
  102.8 2.0 %fusion.124 = f32[256,384]{1,0:T(8,128)} fusion(bf16[256,384]{1,0:T(8,128)(2,1)S(1)} %fusion.50, bf16[1536,384]{1,0:T(8,128)(2,1)} %collective-permute-done.5), kind=kOutput, calls=%fused_computation.134 | convolution fusion | flops 75497472 | bytes 884736 | tf_op jit(solution)/shard_map/dot_general | solution.py:75
  104.8 2.0 %fusion.122 = f32[256,384]{1,0:T(8,128)} fusion(bf16[256,384]{1,0:T(8,128)(2,1)S(1)} %fusion.50, bf16[1536,384]{1,0:T(8,128)(2,1)} %collective-permute-done.5), kind=kOutput, calls=%fused_computation.132 | convolution fusion | flops 75497472 | bytes 884736 | tf_op jit(solution)/shard_map/dot_general | solution.py:75
  106.8 1.5 fusion.74
  108.3 2.0 %fusion.116 = f32[256,384]{1,0:T(8,128)} fusion(bf16[256,384]{1,0:T(8,128)(2,1)S(1)} %fusion.74, bf16[1536,384]{1,0:T(8,128)(2,1)} %collective-permute-done.7), kind=kOutput, calls=%fused_computation.126 | convolution fusion | flops 75497472 | bytes 884736 | tf_op jit(solution)/shard_map/dot_general | solution.py:75
  110.3 2.0 %fusion.114 = f32[256,384]{1,0:T(8,128)} fusion(bf16[256,384]{1,0:T(8,128)(2,1)S(1)} %fusion.74, bf16[1536,384]{1,0:T(8,128)(2,1)} %collective-permute-done.7), kind=kOutput, calls=%fused_computation.124 | convolution fusion | flops 75497472 | bytes 884736 | tf_op jit(solution)/shard_map/dot_general | solution.py:75
  112.3 1.5 fusion.98
  113.8 2.0 %fusion.108 = f32[256,384]{1,0:T(8,128)} fusion(bf16[256,384]{1,0:T(8,128)(2,1)S(1)} %fusion.98, bf16[1536,384]{1,0:T(8,128)(2,1)} %collective-permute-done.9), kind=kOutput, calls=%fused_computation.118 | convolution fusion | flops 75497472 | bytes 884736 | tf_op jit(solution)/shard_map/dot_general | solution.py:75
  115.8 2.0 %fusion.106 = f32[256,384]{1,0:T(8,128)} fusion(bf16[256,384]{1,0:T(8,128)(2,1)S(1)} %fusion.98, bf16[1536,384]{1,0:T(8,128)(2,1)} %collective-permute-done.9), kind=kOutput, calls=%fused_computation.116 | convolution fusion | flops 75497472 | bytes 884736 | tf_op jit(solution)/shard_map/dot_general | solution.py:75
  118.3 1.0 fusion.112
  119.3 1.0 fusion.110
  120.3 4.1 %fusion.164 = (f32[256]{0:T(256)}, f32[256]{0:T(256)}, f32[256,768]{1,0:T(8,128)S(1)}) fusion(f32[768]{0:T(1024)S(1)} %copy-done.22, f32[256,384]{1,0:T(8,128)} %fusion.106, f32[256,384]{1,0:T(8,128)} %fusion.108, f32[256,384]{1,0:T(8,128)} %fusion.110, f32[256,384]{1,0:T(8,128)} %fusion.112, f32[256,384]{1,0:T(8,128)} %fusion.114, ...), kind=kOutput, calls=%fused_computation.213 | convolution fusion | flops 609484288 | bytes 8265728 | tf_op jit(solution)/shard_map/dot_general | solution.py:75
  124.4 0.7 broadcast_multiply_fusion.2
  126.2 0.9 all_to_all.24
  127.1 3.0 %reduce.27 = bf16[256,768]{1,0:T(8,128)(2,1)S(1)} reduce(bf16[256,1,768]{2,1,0:T(2,128)(2,1)S(1)} %all_to_all.24, bf16[]{:T(256)} %broadcast.136), dimensions={1}, to_apply=%all_to_all.24.reduce_sub_computation | reduce | bytes 786434 | tf_op jit(solution)/shard_map/all_to_all | solution.py:229
  130.3 25.4 %all_to_all.28 = bf16[256,2,384]{2,1,0:T(2,128)(2,1)S(1)} all-to-all(bf16[256,2,384]{2,1,0:T(2,128)(2,1)S(1)} %reshape.176), channel_id=1, replica_groups=mesh['seq'=64,'hid'=4] {'hid','seq'}, dimensions={0} | all-to-all | bytes 786432 | tf_op jit(solution)/shard_map/all_to_all | solution.py:229
  156.0 0.7 copy.57
  157.0 0.8 copy.61
  (128 shorter events, 13.5 us)
Async XLA Ops:
  0.0 6.3 %copy-start = (bf16[768,768]{1,0:T(8,128)(2,1)S(1)}, bf16[768,768]{1,0:T(8,128)(2,1)}, u32[]{:S(2)}) copy-start(bf16[768,768]{1,0:T(8,128)(2,1)} %param.21) | copy-start | bytes 3538948
  0.0 6.4 %copy-start.7 = (bf16[768,768]{1,0:T(8,128)(2,1)S(1)}, bf16[768,768]{1,0:T(8,128)(2,1)}, u32[]{:S(2)}) copy-start(bf16[768,768]{1,0:T(8,128)(2,1)} %param.23) | copy-start | bytes 3538948
  1.8 28.9 %collective-permute-start.1 = (f32[9,192]{1,0:T(8,128)S(1)}, f32[9,192]{1,0:T(8,128)S(1)}, u32[]{:S(2)}, u32[]{:S(2)}) collective-permute-start(f32[9,192]{1,0:T(8,128)S(1)} %concatenate.49), channel_id=1, source_target_pairs={{0,3},{1,0},{2,1},{3,2},{4,7},{5,4},{6,5},{7,6},{8,11},{9,8},{10,9... | collective-permute-start | bytes 20744 | tf_op jit(solution)/shard_map/ppermute | solution.py:106
  5.2 25.5 %collective-permute-start.2 = (f32[9,192]{1,0:T(8,128)S(1)}, f32[9,192]{1,0:T(8,128)S(1)}, u32[]{:S(2)}, u32[]{:S(2)}) collective-permute-start(f32[9,192]{1,0:T(8,128)S(1)} %concatenate.49), channel_id=1, source_target_pairs={{0,2},{1,3},{2,0},{3,1},{4,6},{5,7},{6,4},{7,5},{8,10},{9,11},{10,... | collective-permute-start | bytes 20744 | tf_op jit(solution)/shard_map/ppermute | solution.py:106
  5.7 25.0 %collective-permute-start.3 = (f32[9,192]{1,0:T(8,128)S(1)}, f32[9,192]{1,0:T(8,128)S(1)}, u32[]{:S(2)}, u32[]{:S(2)}) collective-permute-start(f32[9,192]{1,0:T(8,128)S(1)} %concatenate.49), channel_id=1, source_target_pairs={{0,1},{1,2},{2,3},{3,0},{4,5},{5,6},{6,7},{7,4},{8,9},{9,10},{10,1... | collective-permute-start | bytes 20744 | tf_op jit(solution)/shard_map/ppermute | solution.py:106
  6.4 3.2 %copy-start.5 = (bf16[1024,192]{0,1:T(8,128)(2,1)S(1)}, bf16[1024,192]{0,1:T(8,128)(2,1)}, u32[]{:S(2)}) copy-start(bf16[1024,192]{0,1:T(8,128)(2,1)} %param.18) | copy-start | bytes 1179652
  6.5 3.2 %copy-start.11 = (bf16[256,256]{1,0:T(8,128)(2,1)S(1)}, bf16[256,256]{1,0:T(8,128)(2,1)}, u32[]{:S(2)}) copy-start(bf16[256,256]{1,0:T(8,128)(2,1)} %constant.103.clone) | copy-start | bytes 393220
  7.6 60.0 %collective-permute-start.4 = (bf16[1536,384]{1,0:T(8,128)(2,1)}, bf16[1536,384]{1,0:T(8,128)(2,1)}, u32[]{:S(2)}, u32[]{:S(2)}) collective-permute-start(bf16[1536,384]{1,0:T(8,128)(2,1)} %pad_maximum_fusion), channel_id=1, source_target_pairs={{0,1},{1,2},{2,3},{3,0},{4,7},{5,4},{6,5},{7,6},{8,9},{9,10},{10,1... | collective-permute-start | bytes 3538952 | tf_op jit(solution)/shard_map/ppermute | solution.py:88
  9.7 60.6 %collective-permute-start.6 = (bf16[1536,384]{1,0:T(8,128)(2,1)}, bf16[1536,384]{1,0:T(8,128)(2,1)}, u32[]{:S(2)}, u32[]{:S(2)}) collective-permute-start(bf16[1536,384]{1,0:T(8,128)(2,1)} %pad_maximum_fusion), channel_id=1, source_target_pairs={{0,3},{1,0},{2,1},{3,2},{4,5},{5,6},{6,7},{7,4},{8,11},{9,8},{10,9... | collective-permute-start | bytes 3538952 | tf_op jit(solution)/shard_map/ppermute | solution.py:88
  12.6 33.2 %all-to-all-start = ((bf16[256,2,384]{2,1,0:T(2,128)(2,1)}), bf16[256,2,384]{2,1,0:T(2,128)(2,1)S(1)}, u32[]{:S(2)}, u32[]{:S(2)}) async-start(bf16[256,2,384]{2,1,0:T(2,128)(2,1)} %reshape.172), calls=%async_computation | async-start | bytes 786432 | tf_op jit(solution)/shard_map/all_to_all | solution.py:171
  30.7 15.1 %copy-start.12 = (f32[9,192]{1,0:T(8,128)}, f32[9,192]{1,0:T(8,128)S(1)}, u32[]{:S(2)}) copy-start(f32[9,192]{1,0:T(8,128)S(1)} %collective-permute-done.3) | copy-start | bytes 20740
  30.8 0.6 copy-start.14
  48.9 1.6 %copy-start.9 = (bf16[512,256]{1,0:T(8,128)(2,1)S(1)}, bf16[512,256]{1,0:T(8,128)(2,1)}, u32[]{:S(2)}) copy-start(bf16[512,256]{1,0:T(8,128)(2,1)} %constant.105.clone) | copy-start | bytes 786436
  53.7 12.0 %copy-start.15 = (f32[8,9,192]{2,1,0:T(8,128)S(1)}, f32[8,9,192]{2,1,0:T(8,128)}, u32[]{:S(2)}) copy-start(f32[8,9,192]{2,1,0:T(8,128)} %copy-done.14) | copy-start | bytes 165892
  53.7 12.1 %copy-start.13 = (f32[9,192]{1,0:T(8,128)S(1)}, f32[9,192]{1,0:T(8,128)}, u32[]{:S(2)}) copy-start(f32[9,192]{1,0:T(8,128)} %copy-done.12) | copy-start | bytes 20740
  55.5 28.4 %all-to-all-start.1 = ((bf16[256,2,384]{2,1,0:T(2,128)(2,1)}), bf16[256,2,384]{2,1,0:T(2,128)(2,1)S(1)}, u32[]{:S(2)}, u32[]{:S(2)}) async-start(bf16[256,2,384]{2,1,0:T(2,128)(2,1)} %reshape.174), calls=%async_computation.1 | async-start | bytes 786432 | tf_op jit(solution)/shard_map/all_to_all | solution.py:189
  67.6 16.8 %copy-start.1 = (f32[256,256]{1,0:T(8,128)S(1)}, f32[256,256]{1,0:T(8,128)}, u32[]{:S(2)}) copy-start(f32[256,256]{1,0:T(8,128)} %constant.109.clone) | copy-start | bytes 786436
  67.6 16.8 %copy-start.2 = (f32[256,256]{1,0:T(8,128)S(1)}, f32[256,256]{1,0:T(8,128)}, u32[]{:S(2)}) copy-start(f32[256,256]{1,0:T(8,128)} %constant.110.clone) | copy-start | bytes 786436
  67.6 16.8 %copy-start.18 = (f32[1,1,256]{2,1,0:T(1,128)S(1)}, f32[1,1,256]{2,1,0:T(1,128)}, u32[]{:S(2)}) copy-start(f32[1,1,256]{2,1,0:T(1,128)} %get-tuple-element.24) | copy-start | bytes 3076
  67.6 16.8 %copy-start.19 = (f32[1,1,256]{2,1,0:T(1,128)S(1)}, f32[1,1,256]{2,1,0:T(1,128)}, u32[]{:S(2)}) copy-start(f32[1,1,256]{2,1,0:T(1,128)} %get-tuple-element.26) | copy-start | bytes 3076
  67.6 16.8 %copy-start.20 = (pred[384]{0:T(512)(128)(4,1)S(1)}, pred[384]{0:T(512)(128)(4,1)}, u32[]{:S(2)}) copy-start(pred[384]{0:T(512)(128)(4,1)} %broadcast_and_fusion) | copy-start | bytes 1156
  67.6 33.3 %collective-permute-start.5 = (bf16[1536,384]{1,0:T(8,128)(2,1)}, bf16[1536,384]{1,0:T(8,128)(2,1)}, u32[]{:S(2)}, u32[]{:S(2)}) collective-permute-start(bf16[1536,384]{1,0:T(8,128)(2,1)} %collective-permute-done.4), channel_id=1, source_target_pairs={{0,1},{1,2},{2,3},{3,0},{4,7},{5,4},{6,5},{7,6},{8,9},{9,10},{10,1... | collective-permute-start | bytes 3538952 | tf_op jit(solution)/shard_map/ppermute | solution.py:88
  70.3 36.5 %collective-permute-start.7 = (bf16[1536,384]{1,0:T(8,128)(2,1)}, bf16[1536,384]{1,0:T(8,128)(2,1)}, u32[]{:S(2)}, u32[]{:S(2)}) collective-permute-start(bf16[1536,384]{1,0:T(8,128)(2,1)} %collective-permute-done.4), channel_id=1, source_target_pairs={{0,4},{4,0},{8,12},{12,8},{16,20},{20,16},{24,28},{28,24},{32,36},... | collective-permute-start | bytes 3538952 | tf_op jit(solution)/shard_map/ppermute | solution.py:92
  70.3 42.0 %collective-permute-start.9 = (bf16[1536,384]{1,0:T(8,128)(2,1)}, bf16[1536,384]{1,0:T(8,128)(2,1)}, u32[]{:S(2)}, u32[]{:S(2)}) collective-permute-start(bf16[1536,384]{1,0:T(8,128)(2,1)} %collective-permute-done.6), channel_id=1, source_target_pairs={{0,4},{4,0},{8,12},{12,8},{16,20},{20,16},{24,28},{28,24},{32,36},... | collective-permute-start | bytes 3538952 | tf_op jit(solution)/shard_map/ppermute | solution.py:92
  84.4 1.2 copy-start.16
  84.4 1.2 copy-start.17
  84.7 1.2 copy-start.29
  84.9 0.9 collective-permute-start
  85.9 1.0 copy-start.8
  86.1 1.0 copy-start.4
  89.9 1.5 copy-start.3
  91.1 1.6 %copy-start.28 = (f32[384]{0:T(512)S(1)}, f32[384]{0:T(512)}, u32[]{:S(2)}) copy-start(f32[384]{0:T(512)} %get-tuple-element.19) | copy-start | bytes 4612
  92.7 25.1 %copy-start.6 = (bf16[256,768]{1,0:T(8,128)(2,1)}, bf16[256,768]{1,0:T(8,128)(2,1)S(1)}, u32[]{:S(2)}) copy-start(bf16[256,768]{1,0:T(8,128)(2,1)S(1)} %add_convert_fusion.1) | copy-start | bytes 1179652
  94.4 2.5 %copy-start.27 = (f32[384]{0:T(512)S(1)}, f32[384]{0:T(512)}, u32[]{:S(2)}) copy-start(f32[384]{0:T(512)} %get-tuple-element.17) | copy-start | bytes 4612
  98.4 2.8 %copy-start.26 = (f32[384]{0:T(512)S(1)}, f32[384]{0:T(512)}, u32[]{:S(2)}) copy-start(f32[384]{0:T(512)} %get-tuple-element.18) | copy-start | bytes 4612
  100.9 16.9 %collective-permute-start.8 = (bf16[1536,384]{1,0:T(8,128)(2,1)}, bf16[1536,384]{1,0:T(8,128)(2,1)S(1)}, u32[]{:S(2)}, u32[]{:S(2)}) collective-permute-start(bf16[1536,384]{1,0:T(8,128)(2,1)} %collective-permute-done.5), channel_id=1, source_target_pairs={{0,4},{4,0},{8,12},{12,8},{16,20},{20,16},{24,28},{28,24},{32,36},... | collective-permute-start | bytes 3538952 | tf_op jit(solution)/shard_map/ppermute | solution.py:92
  102.8 4.0 %copy-start.25 = (f32[384]{0:T(512)S(1)}, f32[384]{0:T(512)}, u32[]{:S(2)}) copy-start(f32[384]{0:T(512)} %get-tuple-element.16) | copy-start | bytes 4612
  108.3 4.0 %copy-start.24 = (f32[384]{0:T(512)S(1)}, f32[384]{0:T(512)}, u32[]{:S(2)}) copy-start(f32[384]{0:T(512)} %get-tuple-element.14) | copy-start | bytes 4612
  113.8 4.0 %copy-start.23 = (f32[384]{0:T(512)S(1)}, f32[384]{0:T(512)}, u32[]{:S(2)}) copy-start(f32[384]{0:T(512)} %get-tuple-element.15) | copy-start | bytes 4612
  118.2 2.0 %copy-start.21 = (f32[768]{0:T(1024)S(1)}, f32[768]{0:T(1024)}, u32[]{:S(2)}) copy-start(f32[768]{0:T(1024)} %param.22) | copy-start | bytes 9220
  118.3 2.0 %copy-start.22 = (f32[768]{0:T(1024)S(1)}, f32[768]{0:T(1024)}, u32[]{:S(2)}) copy-start(f32[768]{0:T(1024)} %add.360) | copy-start | bytes 9220
  155.7 1.0 copy-start.10
where the time goes:
time: 159 us; the launch traced here: 158 us
  starting transfers between devices  35.9 us (23%)
  matrix products  35.1 us (22%)
  waiting for transfers between devices  27.6 us (17%)
  blocking collectives  25.4 us (16%)
  local copies, waits for them, and re-layouts  17.7 us (11%)
  other arithmetic  15.3 us (10%)
    dot_general x25, matrix products, dot(): return jnp.dot(left, right, preferred_element_type=jnp.float32)  34.6 us
    all_to_all x2, waiting for transfers between devices, shards(): taken = lax.all_to_all(sent, EVERY, 0, 0, tiled=True)  27.5 us
    all_to_all x1, blocking collectives, shards(): taken = lax.all_to_all(sent, EVERY, 0, 0, tiled=True)  25.4 us
    all_to_all x2, starting transfers between devices, shards(): taken = lax.all_to_all(sent, EVERY, 0, 0, tiled=True)  25.1 us
    all_to_all x3, other arithmetic, shards(): taken = lax.all_to_all(sent, EVERY, 0, 0, tiled=True)  6.36 us
    ppermute x3, starting transfers between devices, ring(): return lax.ppermute(value, ('seq', 'hid'), pairs)  4.75 us
    unnamed x77, local copies, waits for them, and re-layouts  4.54 us
    ppermute x3, starting transfers between devices, shift_hid(): return lax.ppermute(value, 'hid', pairs)  4.51 us
  transfers between devices with their start and end apart: 12, of which 2 were waited for; matrix products, arithmetic and copies ran while one was open for 32% of the time, Pallas kernels for 0%

commit v1 on v0

v1 whole, which is shorter than its diff:
```python
import math

import jax
import jax.numpy as jnp
import ml_dtypes
import numpy as np
from jax import lax
from jax.experimental import pallas as pl
from jax.experimental.pallas import tpu as pltpu
from jax.sharding import PartitionSpec as P

D = 768
HALF = D // 2
SEQ = 65536
R = 256
SEQ_DEVICES = 64
HID_DEVICES = 4
WIDTH = D // HID_DEVICES
EVERY = ("hid", "seq")
BF16 = ml_dtypes.bfloat16


def residues():
    place = np.arange(R)
    hid, seq = place // SEQ_DEVICES, place % SEQ_DEVICES
    chip = (seq >> 1) * HID_DEVICES + hid
    core = seq & 1
    return np.where(core == 0, chip, np.where(chip == 0, R // 2, R - chip)), chip, core


RESIDUE, CHIP, CORE = residues()
ROW = np.arange(R)
HIGH = 4 * (ROW % 128 // 2) + 2 * (ROW % 2) + ROW // 128


def cosine_sine(phase, period):
    angle = 2.0 * np.pi * (phase % period).astype(np.float64) / period
    return np.cos(angle), np.sin(angle)


def feature_table():
    rows = np.arange(D, dtype=np.int64)[:, None]
    columns = np.arange(HALF + 1, dtype=np.int64)[None, :]
    angle = np.float32(2.0 * math.pi / D) * (rows * columns % D).astype(np.float32)
    cosine = np.cos(angle.astype(np.float64)).astype(BF16)
    sine = (-np.sin(angle.astype(np.float64))).astype(BF16)
    sine[:, 0] = cosine[:, HALF]
    return np.concatenate([cosine[:, :HALF], sine[:, :HALF]], axis=1)


def pairs_of_rows(even, odd):
    return np.stack([even, odd], axis=1).reshape(2 * even.shape[0], -1)


def high_table():
    cosine, sine = cosine_sine(RESIDUE[:, None] * HIGH[None, :], R)
    even = np.concatenate([cosine, sine], axis=1)
    odd = np.concatenate([-sine, cosine], axis=1)
    return pairs_of_rows(even, odd).astype(BF16)


def low_tables():
    cosine, sine = cosine_sine(HIGH[:, None] * RESIDUE[None, :], R)
    table = np.stack([pairs_of_rows(cosine.T, sine.T).T, pairs_of_rows(-sine.T, cosine.T).T])
    own = cosine_sine(RESIDUE[:, None] * RESIDUE[None, :], SEQ)
    other = cosine_sine((R - RESIDUE)[:, None] % R * RESIDUE[None, :], SEQ)
    sign = np.where(np.arange(2 * R) % 2 == 0, 1.0, -1.0)
    turn = [np.repeat(each, 2, axis=1) for each in own]
    turn += [np.repeat(each, 2, axis=1) * sign for each in other]
    return table.astype(np.float32), np.stack(turn, axis=1).astype(np.float32)


FEATURE = feature_table()
HIGH_TABLE = high_table()
LOW_TABLE, LOW_TURN = low_tables()
LANE = np.arange(HALF)
MIRROR = (LANE[:, None] == (HALF - LANE[None, :]) % HALF).astype(BF16)


def dot(left, right):
    return jnp.dot(left, right, preferred_element_type=jnp.float32)


def norm_rows(values, gain, shift):
    mean = jnp.mean(values, axis=1, keepdims=True)
    spread = jnp.mean(values * values, axis=1, keepdims=True) - mean * mean
    return (values - mean) * lax.rsqrt(spread + 1e-05) * gain + shift


def residue_of(place):
    hid, seq = place // SEQ_DEVICES, place % SEQ_DEVICES
    chip = seq // 2 * HID_DEVICES + hid
    late = jnp.where(chip == 0, R // 2, R - chip)
    return jnp.where(seq % 2 == 0, chip, late)


def spread_matrix():
    pair = lax.broadcasted_iota(jnp.int32, (2 * R, 1), 0)
    target = pair % 2 * R + residue_of(pair // 2)
    column = lax.broadcasted_iota(jnp.int32, (1, 2 * R), 1)
    return jnp.where(target == column, 1.0, 0.0).astype(jnp.bfloat16)


def scatter_kernel(tokens_ref, out_ref, wide_ref):
    for a in range(4):
        s, u = divmod(a, 2)
        wide_ref[pl.ds(u * WIDTH, WIDTH), pl.ds(s * R, R)] = tokens_ref[:, pl.ds(a * R, R)]
    out_ref[...] = lax.dot_general(
        spread_matrix(),
        wide_ref[...],
        (((1,), (1,)), ((), ())),
        preferred_element_type=jnp.float32,
    ).astype(out_ref.dtype)


def gather_kernel(taken_ref, out_ref):
    ordered = lax.dot_general(
        taken_ref[...],
        spread_matrix(),
        (((0,), (0,)), ((), ())),
        preferred_element_type=jnp.float32,
    ).astype(out_ref.dtype)
    for a in range(4):
        s, u = divmod(a, 2)
        out_ref[:, pl.ds(a * R, R)] = ordered[u * WIDTH : (u + 1) * WIDTH, s * R : (s + 1) * R]


def high_kernel(
    taken_ref, feature_ref, table_ref, kept_ref, out_ref, local_ref, stacked_ref, semaphore
):
    for hid in range(4):
        for u in range(2):
            local_ref[pl.ds(u * 128, 128), pl.ds(hid * WIDTH, WIDTH)] = taken_ref[
                pl.ds(hid * 128, 128), pl.ds(u * WIDTH, WIDTH)
            ]
    keep = pltpu.make_async_copy(local_ref, kept_ref, semaphore)
    keep.start()
    features = dot(local_ref[...], feature_ref[...])
    stacked_ref[pl.ds(0, R), pl.ds(0, HALF)] = features[:, :HALF].astype(jnp.bfloat16)
    stacked_ref[pl.ds(R, R), pl.ds(0, HALF)] = features[:, HALF:].astype(jnp.bfloat16)
    lane = lax.broadcasted_iota(jnp.int32, (R, 128), 1)
    first, middle = features[:, 0:1], features[:, HALF : HALF + 1]
    above = jnp.where(lane == 0, first, jnp.where(lane == 1, middle, 0.0))
    below = jnp.where(lane == 2, middle, 0.0)
    stacked_ref[pl.ds(0, R), pl.ds(HALF, 128)] = above.astype(jnp.bfloat16)
    stacked_ref[pl.ds(R, R), pl.ds(HALF, 128)] = below.astype(jnp.bfloat16)
    turned = dot(table_ref[...], stacked_ref[...])
    pair = lax.broadcasted_iota(jnp.int32, (2 * R, 128), 0)
    lane = lax.broadcasted_iota(jnp.int32, (2 * R, 128), 1)
    place = pair // 2
    alone = place < 2
    edge = turned[:, HALF:]
    single = jnp.where(jnp.logical_and(alone, pair % 2 == 1), edge[:, 2:3], edge[:, 0:1])
    single = jnp.where(jnp.logical_and(~alone, place % 2 == 1), edge[:, 1:2], single)
    out_ref[:, pl.ds(0, 128)] = jnp.where(lane == 0, single, turned[:, :128]).astype(out_ref.dtype)
    out_ref[:, pl.ds(128, HALF - 128)] = turned[:, 128:HALF].astype(out_ref.dtype)
    keep.wait()


def turn_kernel(turns_ref, table_ref, out_ref, turn_ref, semaphore):
    place = lax.axis_index("hid") * SEQ_DEVICES + lax.axis_index("seq")
    copy = pltpu.make_async_copy(turns_ref.at[place], turn_ref, semaphore)
    copy.start()
    copy.wait()
    for index in range(2):
        matrix = (
            table_ref[0] * turn_ref[pl.ds(2 * index, 1), :]
            + table_ref[1] * turn_ref[pl.ds(2 * index + 1, 1), :]
        )
        out_ref[index] = matrix.astype(out_ref.dtype)


def low_kernel(taken_ref, matrix_ref, own_ref, other_ref, wide_ref):
    scale = 1.0 / math.sqrt(SEQ * D)
    alone = jnp.logical_and(lax.axis_index("hid") == 0, lax.axis_index("seq") < 2)
    wide_ref[:, pl.ds(0, HALF)] = taken_ref[...]
    edge = taken_ref[:, pl.ds(0, 128)].astype(jnp.float32)
    row = lax.broadcasted_iota(jnp.int32, (2 * R, 128), 0)
    lane = lax.broadcasted_iota(jnp.int32, (2 * R, 128), 1)
    raised = pltpu.roll(pltpu.roll(edge, 2 * R - 1, 0), 1, 1)
    edge = jnp.where(row % 2 == 0, jnp.where(lane == 0, edge, raised), 0.0)
    wide_ref[:, pl.ds(HALF, 128)] = edge.astype(wide_ref.dtype)
    lane = lax.broadcasted_iota(jnp.int32, (R, 128), 1)
    single = jnp.logical_and(lane == 0, alone)
    for index, out_ref in enumerate((own_ref, other_ref)):
        usual = dot(matrix_ref[index], wide_ref[...]) * scale
        edge = usual[:, HALF + index : HALF + index + 1]
        out_ref[:, pl.ds(0, 128)] = jnp.where(single, edge, usual[:, :128]).astype(out_ref.dtype)
        out_ref[:, pl.ds(128, HALF - 128)] = usual[:, 128:HALF].astype(out_ref.dtype)


def layer_kernel(
    own_any,
    received_any,
    mirror_any,
    local_any,
    small_refs,
    inner_ref,
    outer_ref,
    ring_refs,
    swapped_refs,
    out_ref,
    own_ref,
    received_ref,
    mirror_ref,
    local_ref,
    around_ref,
    weights_ref,
    rows_ref,
    total_ref,
    semaphores,
):
    hid, seq = lax.axis_index("hid"), lax.axis_index("seq")
    core = lax.rem(seq, 2)
    crossed = jnp.logical_and(core == 1, jnp.logical_or(hid > 0, seq >= 2))

    def copy(source, target, index):
        return pltpu.make_async_copy(source, target, semaphores.at[index])

    inputs = [
        copy(received_any, received_ref, 0),
        copy(mirror_any, mirror_ref, 1),
        copy(own_any, own_ref, 2),
        copy(local_any, local_ref, 3),
    ]
    inputs += [copy(each, around_ref.at[at], 4 + at) for at, each in enumerate(small_refs)]
    for each in inputs:
        each.start()
    inner_from = [(inner_ref, inner_ref)] + [(ring_refs[i], swapped_refs[i]) for i in (0, 2, 1)]
    outer_from = [(outer_ref, outer_ref)] + [
        (swapped_refs[j], ring_refs[j]) for j in (2, 0, 1)
    ]
    sources = [each for pair in zip(inner_from, outer_from) for each in pair]

    @pl.when(core == 0)
    def _():
        for index, each in enumerate(sources):
            copy(each[0], weights_ref.at[index], 8 + index).start()

    @pl.when(core == 1)
    def _():
        for index, each in enumerate(sources):
            copy(each[1], weights_ref.at[index], 8 + index).start()

    for each in inputs:
        each.wait()
    for block in range(4):
        at = lax.rem(block - hid + 4, 4)
        rows_ref[:, pl.ds(block * WIDTH, WIDTH)] = around_ref[at][:, :WIDTH]

    received = received_ref[...]
    own = own_ref[...]
    lane = lax.broadcasted_iota(jnp.int32, (R, HALF), 1)
    take = jnp.logical_and(lane == 0, crossed)
    low = jnp.where(take, received.astype(jnp.float32), own)
    high = jnp.where(take, own, dot(received, mirror_ref[...]))
    mixed = jnp.concatenate([low, high], axis=1)
    first_sum = local_ref[...].astype(jnp.float32) + mixed
    normed = norm_rows(first_sum, rows_ref[0:1, :], rows_ref[1:2, :]).astype(jnp.bfloat16)
    total_ref[...] = normed.astype(jnp.float32) + rows_ref[2:3, :]
    for index, distance in enumerate((0, 3, 1, 2)):
        for at in (2 * index, 2 * index + 1):
            copy(sources[at][0], weights_ref.at[at], 8 + at).wait()
        inner = dot(normed, weights_ref[2 * index]) + around_ref[distance, pl.ds(5, 1), :]
        active = jax.nn.gelu(inner, approximate=True).astype(jnp.bfloat16)
        total_ref[...] += dot(active, weights_ref[2 * index + 1])
    finished = norm_rows(total_ref[...], rows_ref[3:4, :], rows_ref[4:5, :]).astype(out_ref.dtype)
    for block in range(4):
        for u in range(2):
            out_ref[pl.ds(block * 128, 128), pl.ds(u * WIDTH, WIDTH)] = finished[
                u * 128 : (u + 1) * 128, block * WIDTH : (block + 1) * WIDTH
            ]


VMEM = pl.BlockSpec(memory_space=pltpu.VMEM)
HBM = pl.BlockSpec(memory_space=pltpu.HBM)
ANYWHERE = pl.BlockSpec(memory_space=pl.ANY)
PARAMS = pltpu.CompilerParams(vmem_limit_bytes=40 * 2**20)


def array(shape, dtype=jnp.bfloat16):
    return jax.ShapeDtypeStruct(shape, dtype)


def pair_index(seq, hid):
    return seq * HID_DEVICES + hid % HID_DEVICES


def ring(value, sign):
    pairs = []
    for seq in range(SEQ_DEVICES):
        step = -sign if seq & 1 else sign
        for hid in range(HID_DEVICES):
            pairs.append((pair_index(seq, hid), pair_index(seq, hid + step)))
    return lax.ppermute(value, ("seq", "hid"), pairs)


def swap_cores(value):
    return lax.ppermute(value, "seq", [(seq, seq ^ 1) for seq in range(SEQ_DEVICES)])


def swap_mirrored(value):
    pairs = []
    for seq in range(SEQ_DEVICES):
        for hid in range(HID_DEVICES):
            alone = seq < 2 and hid == 0
            pairs.append((pair_index(seq, hid), pair_index(seq if alone else seq ^ 1, hid)))
    return lax.ppermute(value, ("seq", "hid"), pairs)


def shift_hid(value, step):
    pairs = [(hid, (hid + step) % HID_DEVICES) for hid in range(HID_DEVICES)]
    return lax.ppermute(value, "hid", pairs)


def shards(
    tokens,
    first_gain,
    first_shift,
    inner_weight,
    inner_bias,
    outer_weight,
    outer_bias,
    second_gain,
    second_shift,
):
    bf16 = jnp.bfloat16
    f32 = jnp.float32
    core = lax.axis_index("seq") & 1

    payload = jnp.where(core == 0, inner_weight, outer_weight)
    ring_one = ring(payload, 1)
    ring_three = ring(payload, -1)

    tokens_t, _ = lax.optimization_barrier((tokens.T, payload))
    sent = pl.pallas_call(
        scatter_kernel,
        out_shape=array((2 * R, HALF)),
        in_specs=[VMEM],
        out_specs=VMEM,
        scratch_shapes=[pltpu.VMEM((HALF, 2 * R), bf16)],
        compiler_params=PARAMS,
    )(tokens_t)
    taken = lax.all_to_all(sent, EVERY, 0, 0, tiled=True)

    vectors = (first_gain, first_shift, outer_bias, second_gain, second_shift)
    vectors, _ = lax.optimization_barrier(((*vectors, inner_bias), sent))
    small = jnp.stack([jnp.pad(each, (0, D - each.shape[0])) for each in vectors])
    small = jnp.concatenate([small, jnp.zeros((2, D), f32)])
    around = [small, shift_hid(small, -1), shift_hid(small, 2), shift_hid(small, 1)]
    taken, _ = lax.optimization_barrier((taken, around))

    local, sent = pl.pallas_call(
        high_kernel,
        out_shape=(array((R, D)), array((2 * R, HALF))),
        in_specs=[VMEM] * 3,
        out_specs=(HBM, VMEM),
        scratch_shapes=[
            pltpu.VMEM((R, D), bf16),
            pltpu.VMEM((2 * R, 2 * R), bf16),
            pltpu.SemaphoreType.DMA,
        ],
        compiler_params=PARAMS,
    )(taken, jnp.asarray(FEATURE), jnp.asarray(HIGH_TABLE))
    taken = lax.all_to_all(sent, EVERY, 0, 0, tiled=True)

    (ring_one, ring_three), _ = lax.optimization_barrier(((ring_one, ring_three), sent))
    ring_two = ring(ring_one, 1)
    swap_one, swap_three = swap_cores(ring_one), swap_cores(ring_three)
    turns, _ = lax.optimization_barrier((jnp.asarray(LOW_TURN), sent))
    matrices = pl.pallas_call(
        turn_kernel,
        out_shape=array((2, R, 2 * R)),
        in_specs=[HBM, VMEM],
        out_specs=VMEM,
        scratch_shapes=[pltpu.VMEM((4, 2 * R), f32), pltpu.SemaphoreType.DMA],
        compiler_params=PARAMS,
    )(turns, jnp.asarray(LOW_TABLE))
    taken, _ = lax.optimization_barrier((taken, matrices))

    own, other = pl.pallas_call(
        low_kernel,
        out_shape=(array((R, HALF), f32), array((R, HALF))),
        in_specs=[VMEM] * 2,
        out_specs=(VMEM, VMEM),
        scratch_shapes=[pltpu.VMEM((2 * R, 2 * R), bf16)],
        compiler_params=PARAMS,
    )(taken, matrices)
    ring_two_there, _ = lax.optimization_barrier((ring_two, taken))
    swap_two = swap_cores(ring_two_there)
    received = swap_mirrored(other)

    def layer(*refs):
        return layer_kernel(*refs[:4], refs[4:8], *refs[8:10], refs[10:13], refs[13:16], *refs[16:])

    sent = pl.pallas_call(
        layer,
        out_shape=array((2 * R, HALF)),
        in_specs=[ANYWHERE] * 16,
        out_specs=VMEM,
        scratch_shapes=[
            pltpu.VMEM((R, HALF), f32),
            pltpu.VMEM((R, HALF), bf16),
            pltpu.VMEM((HALF, HALF), bf16),
            pltpu.VMEM((R, D), bf16),
            pltpu.VMEM((4, 8, D), f32),
            pltpu.VMEM((8, D, D), bf16),
            pltpu.VMEM((8, D), f32),
            pltpu.VMEM((R, D), f32),
            pltpu.SemaphoreType.DMA((16,)),
        ],
        compiler_params=PARAMS,
    )(
        own,
        received,
        jnp.asarray(MIRROR),
        local,
        *around,
        inner_weight,
        outer_weight,
        ring_one,
        ring_two,
        ring_three,
        swap_one,
        swap_two,
        swap_three,
    )
    taken = lax.all_to_all(sent, EVERY, 0, 0, tiled=True)

    return pl.pallas_call(
        gather_kernel,
        out_shape=array(tokens.shape[::-1]),
        in_specs=[VMEM],
        out_specs=VMEM,
        compiler_params=PARAMS,
    )(taken).T


def solution(mesh):
    return jax.shard_map(
        shards,
        mesh=mesh,
        in_specs=(
            P("seq", "hid"),
            P("hid"),
            P("hid"),
            P(None, "hid"),
            P("hid"),
            P("hid", None),
            P("hid"),
            P("hid"),
            P("hid"),
        ),
        out_specs=P("seq", "hid"),
        check_vma=False,
    )
```

time: 159 us -> 113 us (0.71)
  matrix products: 35.1 us -> 0 us
  other arithmetic: 15.3 us -> 2.46 us
  local copies, waits for them, and re-layouts: 17.7 us -> 6.82 us
  Pallas kernels: 0 us -> 9.97 us
  starting transfers between devices: 35.9 us -> 41.2 us
    dot_general x26 -> x0, matrix products: 34.8 us -> none  [the longest x25 34.6 us: dot(): return jnp.dot(left, right, preferred_element_type=jnp.float32)]
    pallas_call x0 -> x6, Pallas kernels: none -> 9.97 us  [the longest x1 6.15 us: shards(): pl.pallas_call(layer, out_shape=array((2 * R, HALF)), in_specs=[ANYWHERE]...]
    all_to_all x3 -> x0, other arithmetic: 6.36 us -> none  [shards(): taken = lax.all_to_all(sent, EVERY, 0, 0, tiled=True)]
    reshape x8 -> x0, local copies, waits for them, and re-layouts: 4.35 us -> none  [the longest x1 1.21 us: shards(): local = jnp.transpose(local, (2, 1, 0, 3)).reshape(R, D)]
    concatenate x5 -> x0, other arithmetic: 3.96 us -> none  [the longest x3 1.89 us: shards(): sent = jnp.concatenate([spectrum_real, spectrum_imag], axis=1).astype(bf16)]
    concatenate x2 -> x1, local copies, waits for them, and re-layouts: 2.73 us -> 0.05 us  [shards(): small = jnp.concatenate([small, jnp.zeros((2, D), f32)])]
    select_n x0 -> x1, other arithmetic: none -> 2.46 us  [shards(): payload = jnp.where(core == 0, inner_weight, outer_weight)]
    all_to_all x2, starting transfers between devices: 25.1 us -> 27.5 us  [shards(): taken = lax.all_to_all(sent, EVERY, 0, 0, tiled=True)]
  transfers between devices with their start and end apart: 12 -> 12, of which waited for: 2 -> 3; matrix products, arithmetic and copies ran while one was open for 32% -> 0% of each run, Pallas kernels for 0% -> 2%
where the time goes in v1:
time: 113 us
  starting transfers between devices  41.2 us (36%)
  waiting for transfers between devices  28 us (25%)
  blocking collectives  24.2 us (21%)
  Pallas kernels  9.97 us (9%)
  local copies, waits for them, and re-layouts  6.82 us (6%)
  other arithmetic  2.46 us (2%)
    all_to_all x2, starting transfers between devices, shards(): taken = lax.all_to_all(sent, EVERY, 0, 0, tiled=True)  27.5 us
    all_to_all x2, waiting for transfers between devices, shards(): taken = lax.all_to_all(sent, EVERY, 0, 0, tiled=True)  26.3 us
    all_to_all x1, blocking collectives, shards(): taken = lax.all_to_all(sent, EVERY, 0, 0, tiled=True)  24.2 us
    pallas_call x1, Pallas kernels, shards(): pl.pallas_call(layer, out_shape=array((2 * R, HALF)), in_specs=[ANYWHERE]...  6.15 us
    ppermute x3, starting transfers between devices, ring(): return lax.ppermute(value, ('seq', 'hid'), pairs)  5.48 us
    ppermute x3, starting transfers between devices, shift_hid(): return lax.ppermute(value, 'hid', pairs)  5.04 us
    all_to_all x6, local copies, waits for them, and re-layouts, shards(): taken = lax.all_to_all(sent, EVERY, 0, 0, tiled=True)  3.37 us
    unnamed x32, local copies, waits for them, and re-layouts  3.35 us
  transfers between devices with their start and end apart: 12, of which 3 were waited for; matrix products, arithmetic and copies ran while one was open for 0% of the time, Pallas kernels for 2%

profile of v1, /device:TPU:1, one launch (start us, length us, event | category | flops | bytes accessed | tf_op | source)
XLA Modules:
  0.0 113.1 jit_solution(7884279728423366672)
XLA Ops:
  0.0 2.5 %broadcast_select_fusion = bf16[768,768]{1,0:T(8,128)(2,1)} fusion(bf16[768,768]{1,0:T(8,128)(2,1)} %refs_8_.1, bf16[768,768]{1,0:T(8,128)(2,1)} %refs_9_.1, pred[]{:T(512)S(6)} %eq.3), kind=kLoop, calls=%fused_computation | loop fusion | flops 589824 | bytes 3538945 | tf_op jit(solution)/shard_map/jit(_where)/select_n | solution.py:331
  2.5 2.0 %collective-permute-start.5 = (bf16[768,768]{1,0:T(8,128)(2,1)}, bf16[768,768]{1,0:T(8,128)(2,1)}, u32[]{:S(2)}, u32[]{:S(2)}) collective-permute-start(bf16[768,768]{1,0:T(8,128)(2,1)} %broadcast_select_fusion), channel_id=1, source_target_pairs={{0,3},{1,0},{2,1},{3,2},{4,5},{5,6},{6,7},{7,4},{8,11},{9,8},{10,9... | collective-permute-start | bytes 3538952 | tf_op jit(solution)/shard_map/ppermute | solution.py:295
  4.5 1.3 %collective-permute-start.4 = (bf16[768,768]{1,0:T(8,128)(2,1)}, bf16[768,768]{1,0:T(8,128)(2,1)}, u32[]{:S(2)}, u32[]{:S(2)}) collective-permute-start(bf16[768,768]{1,0:T(8,128)(2,1)} %broadcast_select_fusion), channel_id=1, source_target_pairs={{0,1},{1,2},{2,3},{3,0},{4,7},{5,4},{6,5},{7,6},{8,9},{9,10},{10,1... | collective-permute-start | bytes 3538952 | tf_op jit(solution)/shard_map/ppermute | solution.py:295
  5.8 0.0 copy-start.13
  5.8 0.0 copy-start.14
  5.8 0.0 copy-start.15
  5.8 0.5 shard_map.136
  6.3 0.0 copy-start.3
  6.3 0.0 copy-start.5
  6.4 0.9 all_to_all.23
  7.2 15.3 %all-to-all-start = ((bf16[256,2,384]{2,1,0:T(2,128)(2,1)}), bf16[256,2,384]{2,1,0:T(2,128)(2,1)S(1)}, u32[]{:S(2)}, u32[]{:S(2)}) async-start(bf16[256,2,384]{2,1,0:T(2,128)(2,1)} %all_to_all.23), calls=%async_computation | async-start | bytes 786432 | tf_op jit(solution)/shard_map/all_to_all | solution.py:344
  22.8 1.5 %collective-permute-start.2 = (f32[8,768]{1,0:T(8,128)S(1)}, f32[8,768]{1,0:T(8,128)S(1)}, u32[]{:S(2)}, u32[]{:S(2)}) collective-permute-start(f32[8,768]{1,0:T(8,128)S(1)} %concatenate.3.refs_4_), channel_id=1, source_target_pairs={{0,1},{1,2},{2,3},{3,0},{4,5},{5,6},{6,7},{7,4},{8,9},{9,10},{10,1... | collective-permute-start | bytes 73736 | tf_op jit(solution)/shard_map/ppermute | solution.py:313
  24.3 2.4 %collective-permute-start.1 = (f32[8,768]{1,0:T(8,128)S(1)}, f32[8,768]{1,0:T(8,128)S(1)}, u32[]{:S(2)}, u32[]{:S(2)}) collective-permute-start(f32[8,768]{1,0:T(8,128)S(1)} %concatenate.3.refs_4_), channel_id=1, source_target_pairs={{0,2},{1,3},{2,0},{3,1},{4,6},{5,7},{6,4},{7,5},{8,10},{9,11},{10,... | collective-permute-start | bytes 73736 | tf_op jit(solution)/shard_map/ppermute | solution.py:313
  26.7 1.2 %collective-permute-start = (f32[8,768]{1,0:T(8,128)S(1)}, f32[8,768]{1,0:T(8,128)S(1)}, u32[]{:S(2)}, u32[]{:S(2)}) collective-permute-start(f32[8,768]{1,0:T(8,128)S(1)} %concatenate.3.refs_4_), channel_id=1, source_target_pairs={{0,3},{1,0},{2,1},{3,2},{4,7},{5,4},{6,5},{7,6},{8,11},{9,8},{10,9... | collective-permute-start | bytes 73736 | tf_op jit(solution)/shard_map/ppermute | solution.py:313
  27.9 13.0 %all-to-all-done = bf16[256,2,384]{2,1,0:T(2,128)(2,1)S(1)} async-done(((bf16[256,2,384]{2,1,0:T(2,128)(2,1)}), bf16[256,2,384]{2,1,0:T(2,128)(2,1)S(1)}, u32[]{:S(2)}, u32[]{:S(2)}) %all-to-all-start) | async-done | bytes 393248 | tf_op jit(solution)/shard_map/all_to_all | solution.py:344
  40.9 0.1 all_to_all.25.taken_ref
  41.0 0.0 collective-permute-done.2.refs_7_
  41.0 0.0 collective-permute-done.1.refs_6_
  41.0 0.0 collective-permute-done.refs_5_
  41.1 1.4 %shard_map.137 = (bf16[256,768]{1,0:T(8,128)(2,1)S(1)}, bf16[512,384]{1,0:T(8,128)(2,1)S(1)}) custom-call(bf16[512,384]{1,0:T(8,128)(2,1)S(1)} %all_to_all.25.taken_ref, bf16[768,768]{1,0:T(8,128)(2,1)S(1)} %copy-done.3, bf16[512,512]{1,0:T(8,128)(2,1)S(1)} %copy-done.5), custom_call_target="tpu_custom_call" | custom-call | tf_op jit(solution)/shard_map/pallas_call | solution.py:353
  42.5 0.7 copy-done.6
  43.2 0.0 collective-permute-done.5.refs_12_
  43.2 0.0 collective-permute-done.4.refs_10_
  43.2 2.2 %collective-permute-start.6 = (bf16[768,768]{1,0:T(8,128)(2,1)}, bf16[768,768]{1,0:T(8,128)(2,1)}, u32[]{:S(2)}, u32[]{:S(2)}) collective-permute-start(bf16[768,768]{1,0:T(8,128)(2,1)} %collective-permute-done.4.refs_10_), channel_id=1, source_target_pairs={{0,1},{1,2},{2,3},{3,0},{4,7},{5,4},{6,5},{7,6},{8,9},{9,10},{10,1... | collective-permute-start | bytes 3538952 | tf_op jit(solution)/shard_map/ppermute | solution.py:295
  45.4 0.9 all_to_all.26
  46.3 12.2 %all-to-all-start.1 = ((bf16[256,2,384]{2,1,0:T(2,128)(2,1)}), bf16[256,2,384]{2,1,0:T(2,128)(2,1)}, u32[]{:S(2)}, u32[]{:S(2)}) async-start(bf16[256,2,384]{2,1,0:T(2,128)(2,1)} %all_to_all.26), calls=%async_computation.1 | async-start | bytes 786432 | tf_op jit(solution)/shard_map/all_to_all | solution.py:365
  58.5 0.0 copy-start.2
  58.5 1.6 %copy-done.2 = f32[256,4,512]{2,1,0:T(4,128)S(1)} copy-done((f32[256,4,512]{2,1,0:T(4,128)S(1)}, f32[256,4,512]{2,1,0:T(4,128)}, u32[]{:S(2)}) %copy-start.2) | copy-done | bytes 2097176
  60.1 0.1 shard_map.138.matrix_ref
  60.2 0.0 copy-start
  60.2 2.3 %collective-permute-start.7 = (bf16[768,768]{1,0:T(8,128)(2,1)}, bf16[768,768]{1,0:T(8,128)(2,1)}, u32[]{:S(2)}, u32[]{:S(2)}) collective-permute-start(bf16[768,768]{1,0:T(8,128)(2,1)} %collective-permute-done.4.refs_10_), channel_id=1, source_target_pairs={{0,4},{4,0},{8,12},{12,8},{16,20},{20,16},{24,28},{28,24},{32,36},... | collective-permute-start | bytes 3538952 | tf_op jit(solution)/shard_map/ppermute | solution.py:299
  62.5 0.1 collective-permute-start.9
  62.6 13.3 %all-to-all-done.1 = bf16[256,2,384]{2,1,0:T(2,128)(2,1)} async-done(((bf16[256,2,384]{2,1,0:T(2,128)(2,1)}), bf16[256,2,384]{2,1,0:T(2,128)(2,1)}, u32[]{:S(2)}, u32[]{:S(2)}) %all-to-all-start.1) | async-done | bytes 393248 | tf_op jit(solution)/shard_map/all_to_all | solution.py:365
  75.9 1.1 %all_to_all.28.taken_ref = bf16[512,384]{1,0:T(8,128)(2,1)S(1)} reshape(bf16[256,2,384]{2,1,0:T(2,128)(2,1)} %all-to-all-done.1) | data formatting | bytes 786432 | tf_op jit(solution)/shard_map/all_to_all | solution.py:365
  77.1 0.0 collective-permute-done.6.refs_11_
  77.1 0.1 collective-permute-start.8
  77.2 0.6 shard_map.139
  77.8 0.7 collective-permute-start.3
  78.5 0.0 collective-permute-done.9.refs_15_
  78.5 0.0 collective-permute-done.7.refs_13_
  78.5 1.7 %collective-permute-done.8.refs_14_ = bf16[768,768]{1,0:T(8,128)(2,1)S(1)} collective-permute-done((bf16[768,768]{1,0:T(8,128)(2,1)}, bf16[768,768]{1,0:T(8,128)(2,1)S(1)}, u32[]{:S(2)}, u32[]{:S(2)}) %collective-permute-start.8) | collective-permute-done | bytes 1179680 | tf_op jit(solution)/shard_map/ppermute | solution.py:299
  80.2 0.0 copy-start.9
  80.3 1.0 copy-done.9
  81.2 6.1 %shard_map.140 = bf16[512,384]{1,0:T(8,128)(2,1)S(1)} custom-call(f32[256,384]{1,0:T(8,128)S(1)} %get-tuple-element.33.refs_0_, bf16[256,384]{1,0:T(8,128)(2,1)S(1)} %collective-permute-done.3.refs_1_, bf16[384,384]{1,0:T(8,128)(2,1)S(1)} %copy-done.9, bf16[256,768]{1,0:T(8,128)(2,1)S(1)} %copy-done.7, f32[8,768]{1,0:T(8,128)S(1)} %concatenate.3.refs_4_, ...), custom_call_target="tpu_custom_call" | custom-call | tf_op jit(solution)/shard_map/pallas_call | solution.py:396
  87.4 0.1 all_to_all.29
  87.5 24.2 %all_to_all.35 = bf16[256,2,384]{2,1,0:T(2,128)(2,1)S(1)} all-to-all(bf16[256,2,384]{2,1,0:T(2,128)(2,1)S(1)} %all_to_all.29), channel_id=1, replica_groups=mesh['seq'=64,'hid'=4] {'hid','seq'}, dimensions={0} | all-to-all | bytes 786432 | tf_op jit(solution)/shard_map/all_to_all | solution.py:428
  111.8 0.1 all_to_all.31.taken_ref
  111.9 1.2 %shard_map.141 = bf16[192,1024]{1,0:T(8,128)(2,1)} custom-call(bf16[512,384]{1,0:T(8,128)(2,1)S(1)} %all_to_all.31.taken_ref), custom_call_target="tpu_custom_call" | custom-call | tf_op jit(solution)/shard_map/pallas_call | solution.py:430
  (35 shorter events, 0.1 us)
Async XLA Ops:
  0.0 5.8 %copy-start.8 = (bf16[1024,192]{0,1:T(8,128)(2,1)S(1)}, bf16[1024,192]{0,1:T(8,128)(2,1)}, u32[]{:S(2)}) copy-start(bf16[1024,192]{0,1:T(8,128)(2,1)} %param.14) | copy-start | bytes 1179652
  2.5 40.8 %collective-permute-start.5 = (bf16[768,768]{1,0:T(8,128)(2,1)}, bf16[768,768]{1,0:T(8,128)(2,1)}, u32[]{:S(2)}, u32[]{:S(2)}) collective-permute-start(bf16[768,768]{1,0:T(8,128)(2,1)} %broadcast_select_fusion), channel_id=1, source_target_pairs={{0,3},{1,0},{2,1},{3,2},{4,5},{5,6},{6,7},{7,4},{8,11},{9,8},{10,9... | collective-permute-start | bytes 3538952 | tf_op jit(solution)/shard_map/ppermute | solution.py:295
  4.5 38.7 %collective-permute-start.4 = (bf16[768,768]{1,0:T(8,128)(2,1)}, bf16[768,768]{1,0:T(8,128)(2,1)}, u32[]{:S(2)}, u32[]{:S(2)}) collective-permute-start(bf16[768,768]{1,0:T(8,128)(2,1)} %broadcast_select_fusion), channel_id=1, source_target_pairs={{0,1},{1,2},{2,3},{3,0},{4,7},{5,4},{6,5},{7,6},{8,9},{9,10},{10,1... | collective-permute-start | bytes 3538952 | tf_op jit(solution)/shard_map/ppermute | solution.py:295
  5.8 16.8 %copy-start.10 = (f32[768]{0:T(1024)S(1)}, f32[768]{0:T(1024)}, u32[]{:S(2)}) copy-start(f32[768]{0:T(1024)} %param.18) | copy-start | bytes 9220
  5.8 16.8 %copy-start.11 = (f32[192]{0:T(256)S(1)}, f32[192]{0:T(256)}, u32[]{:S(2)}) copy-start(f32[192]{0:T(256)} %param.15) | copy-start | bytes 2308
  5.8 16.8 %copy-start.12 = (f32[192]{0:T(256)S(1)}, f32[192]{0:T(256)}, u32[]{:S(2)}) copy-start(f32[192]{0:T(256)} %param.16) | copy-start | bytes 2308
  5.8 16.9 %copy-start.13 = (f32[192]{0:T(256)S(1)}, f32[192]{0:T(256)}, u32[]{:S(2)}) copy-start(f32[192]{0:T(256)} %param.20) | copy-start | bytes 2308
  5.8 16.9 %copy-start.14 = (f32[192]{0:T(256)S(1)}, f32[192]{0:T(256)}, u32[]{:S(2)}) copy-start(f32[192]{0:T(256)} %param.21) | copy-start | bytes 2308
  5.8 16.9 %copy-start.15 = (f32[192]{0:T(256)S(1)}, f32[192]{0:T(256)}, u32[]{:S(2)}) copy-start(f32[192]{0:T(256)} %param.22) | copy-start | bytes 2308
  6.3 34.7 %copy-start.3 = (bf16[768,768]{1,0:T(8,128)(2,1)S(1)}, bf16[768,768]{1,0:T(8,128)(2,1)}, u32[]{:S(2)}) copy-start(bf16[768,768]{1,0:T(8,128)(2,1)} %constant.23.clone.feature_ref) | copy-start | bytes 3538948
  6.3 34.7 %copy-start.5 = (bf16[512,512]{1,0:T(8,128)(2,1)S(1)}, bf16[512,512]{1,0:T(8,128)(2,1)}, u32[]{:S(2)}) copy-start(bf16[512,512]{1,0:T(8,128)(2,1)} %constant.24.clone.table_ref) | copy-start | bytes 1572868
  7.2 33.6 %all-to-all-start = ((bf16[256,2,384]{2,1,0:T(2,128)(2,1)}), bf16[256,2,384]{2,1,0:T(2,128)(2,1)S(1)}, u32[]{:S(2)}, u32[]{:S(2)}) async-start(bf16[256,2,384]{2,1,0:T(2,128)(2,1)} %all_to_all.23), calls=%async_computation | async-start | bytes 786432 | tf_op jit(solution)/shard_map/all_to_all | solution.py:344
  22.8 18.2 %collective-permute-start.2 = (f32[8,768]{1,0:T(8,128)S(1)}, f32[8,768]{1,0:T(8,128)S(1)}, u32[]{:S(2)}, u32[]{:S(2)}) collective-permute-start(f32[8,768]{1,0:T(8,128)S(1)} %concatenate.3.refs_4_), channel_id=1, source_target_pairs={{0,1},{1,2},{2,3},{3,0},{4,5},{5,6},{6,7},{7,4},{8,9},{9,10},{10,1... | collective-permute-start | bytes 73736 | tf_op jit(solution)/shard_map/ppermute | solution.py:313
  24.3 16.7 %collective-permute-start.1 = (f32[8,768]{1,0:T(8,128)S(1)}, f32[8,768]{1,0:T(8,128)S(1)}, u32[]{:S(2)}, u32[]{:S(2)}) collective-permute-start(f32[8,768]{1,0:T(8,128)S(1)} %concatenate.3.refs_4_), channel_id=1, source_target_pairs={{0,2},{1,3},{2,0},{3,1},{4,6},{5,7},{6,4},{7,5},{8,10},{9,11},{10,... | collective-permute-start | bytes 73736 | tf_op jit(solution)/shard_map/ppermute | solution.py:313
  26.7 14.4 %collective-permute-start = (f32[8,768]{1,0:T(8,128)S(1)}, f32[8,768]{1,0:T(8,128)S(1)}, u32[]{:S(2)}, u32[]{:S(2)}) collective-permute-start(f32[8,768]{1,0:T(8,128)S(1)} %concatenate.3.refs_4_), channel_id=1, source_target_pairs={{0,3},{1,0},{2,1},{3,2},{4,7},{5,4},{6,5},{7,6},{8,11},{9,8},{10,9... | collective-permute-start | bytes 73736 | tf_op jit(solution)/shard_map/ppermute | solution.py:313
  42.5 0.7 copy-start.6
  43.2 15.3 %copy-start.4 = (f32[2,256,512]{2,1,0:T(8,128)S(1)}, f32[2,256,512]{2,1,0:T(8,128)}, u32[]{:S(2)}) copy-start(f32[2,256,512]{2,1,0:T(8,128)} %constant.26.clone.table_ref) | copy-start | bytes 3145732
  43.2 33.8 %collective-permute-start.6 = (bf16[768,768]{1,0:T(8,128)(2,1)}, bf16[768,768]{1,0:T(8,128)(2,1)}, u32[]{:S(2)}, u32[]{:S(2)}) collective-permute-start(bf16[768,768]{1,0:T(8,128)(2,1)} %collective-permute-done.4.refs_10_), channel_id=1, source_target_pairs={{0,1},{1,2},{2,3},{3,0},{4,7},{5,4},{6,5},{7,6},{8,9},{9,10},{10,1... | collective-permute-start | bytes 3538952 | tf_op jit(solution)/shard_map/ppermute | solution.py:295
  46.3 29.6 %all-to-all-start.1 = ((bf16[256,2,384]{2,1,0:T(2,128)(2,1)}), bf16[256,2,384]{2,1,0:T(2,128)(2,1)}, u32[]{:S(2)}, u32[]{:S(2)}) async-start(bf16[256,2,384]{2,1,0:T(2,128)(2,1)} %all_to_all.26), calls=%async_computation.1 | async-start | bytes 786432 | tf_op jit(solution)/shard_map/all_to_all | solution.py:365
  58.5 1.6 %copy-start.2 = (f32[256,4,512]{2,1,0:T(4,128)S(1)}, f32[256,4,512]{2,1,0:T(4,128)}, u32[]{:S(2)}) copy-start(f32[256,4,512]{2,1,0:T(4,128)} %constant.25.clone.turns_ref) | copy-start | bytes 6291460
  60.1 20.1 %copy-start.1 = (bf16[768,768]{1,0:T(8,128)(2,1)S(1)}, bf16[768,768]{1,0:T(8,128)(2,1)}, u32[]{:S(2)}) copy-start(bf16[768,768]{1,0:T(8,128)(2,1)} %refs_9_.1) | copy-start | bytes 3538948
  60.2 20.0 %copy-start = (bf16[768,768]{1,0:T(8,128)(2,1)S(1)}, bf16[768,768]{1,0:T(8,128)(2,1)}, u32[]{:S(2)}) copy-start(bf16[768,768]{1,0:T(8,128)(2,1)} %refs_8_.1) | copy-start | bytes 3538948
  60.2 18.2 %collective-permute-start.7 = (bf16[768,768]{1,0:T(8,128)(2,1)}, bf16[768,768]{1,0:T(8,128)(2,1)}, u32[]{:S(2)}, u32[]{:S(2)}) collective-permute-start(bf16[768,768]{1,0:T(8,128)(2,1)} %collective-permute-done.4.refs_10_), channel_id=1, source_target_pairs={{0,4},{4,0},{8,12},{12,8},{16,20},{20,16},{24,28},{28,24},{32,36},... | collective-permute-start | bytes 3538952 | tf_op jit(solution)/shard_map/ppermute | solution.py:299
  62.5 15.9 %collective-permute-start.9 = (bf16[768,768]{1,0:T(8,128)(2,1)}, bf16[768,768]{1,0:T(8,128)(2,1)}, u32[]{:S(2)}, u32[]{:S(2)}) collective-permute-start(bf16[768,768]{1,0:T(8,128)(2,1)} %collective-permute-done.5.refs_12_), channel_id=1, source_target_pairs={{0,4},{4,0},{8,12},{12,8},{16,20},{20,16},{24,28},{28,24},{32,36},... | collective-permute-start | bytes 3538952 | tf_op jit(solution)/shard_map/ppermute | solution.py:299
  77.1 3.2 %copy-start.7 = (bf16[256,768]{1,0:T(8,128)(2,1)S(1)}, bf16[256,768]{1,0:T(8,128)(2,1)}, u32[]{:S(2)}) copy-start(bf16[256,768]{1,0:T(8,128)(2,1)} %copy-done.6) | copy-start | bytes 1179652
  77.1 3.1 %collective-permute-start.8 = (bf16[768,768]{1,0:T(8,128)(2,1)}, bf16[768,768]{1,0:T(8,128)(2,1)S(1)}, u32[]{:S(2)}, u32[]{:S(2)}) collective-permute-start(bf16[768,768]{1,0:T(8,128)(2,1)} %collective-permute-done.6.refs_11_), channel_id=1, source_target_pairs={{0,4},{4,0},{8,12},{12,8},{16,20},{20,16},{24,28},{28,24},{32,36},... | collective-permute-start | bytes 3538952 | tf_op jit(solution)/shard_map/ppermute | solution.py:299
  77.8 0.7 collective-permute-start.3
  80.2 1.0 copy-start.9

commit v2 on v1

--- a/solution.py
+++ b/solution.py
@@ -17,6 +17,7 @@
 HID_DEVICES = 4
 WIDTH = D // HID_DEVICES
 EVERY = ("hid", "seq")
+CHUNKS = (R, 2, HALF)
 BF16 = ml_dtypes.bfloat16
 
 
@@ -59,20 +60,15 @@
     return pairs_of_rows(even, odd).astype(BF16)
 
 
-def low_tables():
+def low_table():
     cosine, sine = cosine_sine(HIGH[:, None] * RESIDUE[None, :], R)
     table = np.stack([pairs_of_rows(cosine.T, sine.T).T, pairs_of_rows(-sine.T, cosine.T).T])
-    own = cosine_sine(RESIDUE[:, None] * RESIDUE[None, :], SEQ)
-    other = cosine_sine((R - RESIDUE)[:, None] % R * RESIDUE[None, :], SEQ)
-    sign = np.where(np.arange(2 * R) % 2 == 0, 1.0, -1.0)
-    turn = [np.repeat(each, 2, axis=1) for each in own]
-    turn += [np.repeat(each, 2, axis=1) * sign for each in other]
-    return table.astype(np.float32), np.stack(turn, axis=1).astype(np.float32)
+    return table.astype(np.float32)
 
 
 FEATURE = feature_table()
 HIGH_TABLE = high_table()
-LOW_TABLE, LOW_TURN = low_tables()
+LOW_TABLE = low_table()
 LANE = np.arange(HALF)
 MIRROR = (LANE[:, None] == (HALF - LANE[None, :]) % HALF).astype(BF16)
 
@@ -101,21 +97,49 @@
     return jnp.where(target == column, 1.0, 0.0).astype(jnp.bfloat16)
 
 
+def payload_kernel(inner_ref, outer_ref, *rest):
+    *vector_refs, payload_ref, rows_ref, semaphore = rest
+    core = lax.rem(lax.axis_index("seq"), 2)
+    weights = payload_ref.at[pl.ds(0, D)]
+
+    @pl.when(core == 0)
+    def _():
+        pltpu.make_async_copy(inner_ref, weights, semaphore).start()
+
+    @pl.when(core == 1)
+    def _():
+        pltpu.make_async_copy(outer_ref, weights, semaphore).start()
+
+    rows_ref[...] = jnp.zeros_like(rows_ref)
+    for index, each in enumerate(vector_refs):
+        row, at = divmod(index, 4) if index < 5 else (2, 0)
+        rows_ref[row : row + 1, pl.ds(at * WIDTH, each.shape[0])] = each[...][None, :]
+    rest = rows_ref[...]
+    pieces = []
+    for _ in range(3):
+        pieces.append(rest.astype(jnp.bfloat16).astype(jnp.float32))
+        rest = rest - pieces[-1]
+    pieces.append(jnp.zeros_like(rest))
+    payload_ref[pl.ds(D, EXTRA), :] = jnp.concatenate(pieces, axis=0).astype(jnp.bfloat16)
+    pltpu.make_async_copy(inner_ref, weights, semaphore).wait()
+
+
 def scatter_kernel(tokens_ref, out_ref, wide_ref):
     for a in range(4):
         s, u = divmod(a, 2)
         wide_ref[pl.ds(u * WIDTH, WIDTH), pl.ds(s * R, R)] = tokens_ref[:, pl.ds(a * R, R)]
-    out_ref[...] = lax.dot_general(
+    spread = lax.dot_general(
         spread_matrix(),
         wide_ref[...],
         (((1,), (1,)), ((), ())),
         preferred_element_type=jnp.float32,
-    ).astype(out_ref.dtype)
+    )
+    out_ref[...] = spread.astype(out_ref.dtype).reshape(out_ref.shape)
 
 
 def gather_kernel(taken_ref, out_ref):
     ordered = lax.dot_general(
-        taken_ref[...],
+        taken_ref[...].reshape(2 * R, HALF),
         spread_matrix(),
         (((0,), (0,)), ((), ())),
         preferred_element_type=jnp.float32,
@@ -125,13 +149,12 @@
         out_ref[:, pl.ds(a * R, R)] = ordered[u * WIDTH : (u + 1) * WIDTH, s * R : (s + 1) * R]
 
 
-def high_kernel(
-    taken_ref, feature_ref, table_ref, kept_ref, out_ref, local_ref, stacked_ref, semaphore
-):
+def high_kernel(taken_ref, feature_ref, table_ref, kept_ref, out_ref, local_ref, stacked_ref, semaphore):
+    taken = taken_ref[...].reshape(2 * R, HALF)
     for hid in range(4):
         for u in range(2):
-            local_ref[pl.ds(u * 128, 128), pl.ds(hid * WIDTH, WIDTH)] = taken_ref[
-                pl.ds(hid * 128, 128), pl.ds(u * WIDTH, WIDTH)
+            local_ref[pl.ds(u * 128, 128), pl.ds(hid * WIDTH, WIDTH)] = taken[
+                hid * 128 : (hid + 1) * 128, u * WIDTH : (u + 1) * WIDTH
             ]
     keep = pltpu.make_async_copy(local_ref, kept_ref, semaphore)
     keep.start()
@@ -147,34 +170,37 @@
     turned = dot(table_ref[...], stacked_ref[...])
     pair = lax.broadcasted_iota(jnp.int32, (2 * R, 128), 0)
     lane = lax.broadcasted_iota(jnp.int32, (2 * R, 128), 1)
-    place = pair // 2
-    alone = place < 2
+    there = pair // 2
+    alone = there < 2
     edge = turned[:, HALF:]
     single = jnp.where(jnp.logical_and(alone, pair % 2 == 1), edge[:, 2:3], edge[:, 0:1])
-    single = jnp.where(jnp.logical_and(~alone, place % 2 == 1), edge[:, 1:2], single)
-    out_ref[:, pl.ds(0, 128)] = jnp.where(lane == 0, single, turned[:, :128]).astype(out_ref.dtype)
-    out_ref[:, pl.ds(128, HALF - 128)] = turned[:, 128:HALF].astype(out_ref.dtype)
+    single = jnp.where(jnp.logical_and(~alone, there % 2 == 1), edge[:, 1:2], single)
+    head = jnp.where(lane == 0, single, turned[:, :128])
+    sent = jnp.concatenate([head, turned[:, 128:HALF]], axis=1)
+    out_ref[...] = sent.astype(out_ref.dtype).reshape(out_ref.shape)
     keep.wait()
 
 
-def turn_kernel(turns_ref, table_ref, out_ref, turn_ref, semaphore):
-    place = lax.axis_index("hid") * SEQ_DEVICES + lax.axis_index("seq")
-    copy = pltpu.make_async_copy(turns_ref.at[place], turn_ref, semaphore)
-    copy.start()
-    copy.wait()
+def turn_kernel(table_ref, out_ref):
+    residue = residue_of(lax.axis_index("hid") * SEQ_DEVICES + lax.axis_index("seq"))
+    column = lax.broadcasted_iota(jnp.int32, (8, 2 * R), 1)
+    opposite = jnp.where(residue == 0, 0, R - residue)
+    row = lax.broadcasted_iota(jnp.int32, (8, 2 * R), 0)
+    phase = jnp.where(row == 0, residue, opposite) * residue_of(column // 2)
+    angle = phase.astype(jnp.float32) * (2.0 * math.pi / SEQ)
+    sign = jnp.where(jnp.logical_or(row == 0, column % 2 == 0), 1.0, -1.0)
+    cosine, sine = jnp.cos(angle) * sign, jnp.sin(angle) * sign
     for index in range(2):
-        matrix = (
-            table_ref[0] * turn_ref[pl.ds(2 * index, 1), :]
-            + table_ref[1] * turn_ref[pl.ds(2 * index + 1, 1), :]
-        )
+        matrix = table_ref[0] * cosine[index : index + 1] + table_ref[1] * sine[index : index + 1]
         out_ref[index] = matrix.astype(out_ref.dtype)
 
 
 def low_kernel(taken_ref, matrix_ref, own_ref, other_ref, wide_ref):
     scale = 1.0 / math.sqrt(SEQ * D)
     alone = jnp.logical_and(lax.axis_index("hid") == 0, lax.axis_index("seq") < 2)
-    wide_ref[:, pl.ds(0, HALF)] = taken_ref[...]
-    edge = taken_ref[:, pl.ds(0, 128)].astype(jnp.float32)
+    taken = taken_ref[...].reshape(2 * R, HALF)
+    wide_ref[:, pl.ds(0, HALF)] = taken
+    edge = taken[:, :128].astype(jnp.float32)
     row = lax.broadcasted_iota(jnp.int32, (2 * R, 128), 0)
     lane = lax.broadcasted_iota(jnp.int32, (2 * R, 128), 1)
     raised = pltpu.roll(pltpu.roll(edge, 2 * R - 1, 0), 1, 1)
@@ -189,14 +215,19 @@
         out_ref[:, pl.ds(128, HALF - 128)] = usual[:, 128:HALF].astype(out_ref.dtype)
 
 
+def whole_rows(parts):
+    parts = parts.astype(jnp.float32)
+    return parts[0:8] + parts[8:16] + parts[16:24]
+
+
 def layer_kernel(
     own_any,
     received_any,
     mirror_any,
     local_any,
-    small_refs,
     inner_ref,
     outer_ref,
+    payload_ref,
     ring_refs,
     swapped_refs,
     out_ref,
@@ -208,6 +239,7 @@
     weights_ref,
     rows_ref,
     total_ref,
+    folded_ref,
     semaphores,
 ):
     hid, seq = lax.axis_index("hid"), lax.axis_index("seq")
@@ -223,30 +255,44 @@
         copy(own_any, own_ref, 2),
         copy(local_any, local_ref, 3),
     ]
-    inputs += [copy(each, around_ref.at[at], 4 + at) for at, each in enumerate(small_refs)]
     for each in inputs:
         each.start()
-    inner_from = [(inner_ref, inner_ref)] + [(ring_refs[i], swapped_refs[i]) for i in (0, 2, 1)]
-    outer_from = [(outer_ref, outer_ref)] + [
-        (swapped_refs[j], ring_refs[j]) for j in (2, 0, 1)
-    ]
+    inner_from = [(inner_ref, inner_ref)]
+    outer_from = [(outer_ref, outer_ref)]
+    small_from = [(payload_ref, payload_ref)]
+    for i, j in ((0, 2), (2, 0), (1, 1)):
+        pair = (ring_refs[i], swapped_refs[i])
+        inner_from.append(tuple(each.at[pl.ds(0, D)] for each in pair))
+        small_from.append(pair)
+        outer_from.append(
+            tuple(each.at[pl.ds(0, D)] for each in (swapped_refs[j], ring_refs[j]))
+        )
     sources = [each for pair in zip(inner_from, outer_from) for each in pair]
 
-    @pl.when(core == 0)
-    def _():
-        for index, each in enumerate(sources):
-            copy(each[0], weights_ref.at[index], 8 + index).start()
-
-    @pl.when(core == 1)
-    def _():
-        for index, each in enumerate(sources):
-            copy(each[1], weights_ref.at[index], 8 + index).start()
-
+    def small_copy(which, taken_by):
+        source = small_from[which][taken_by].at[pl.ds(D, EXTRA)]
+        return copy(source, around_ref.at[(0, 3, 1, 2)[which]], 4 + which)
+
+    for taken_by in range(2):
+
+        @pl.when(core == taken_by)
+        def _():
+            for which in range(4):
+                small_copy(which, taken_by).start()
+            for index, each in enumerate(sources):
+                copy(each[taken_by], weights_ref.at[index], 8 + index).start()
+
+    inputs += [small_copy(which, 0) for which in range(4)]
     for each in inputs:
         each.wait()
     for block in range(4):
         at = lax.rem(block - hid + 4, 4)
-        rows_ref[:, pl.ds(block * WIDTH, WIDTH)] = around_ref[at][:, :WIDTH]
+        sums = whole_rows(around_ref[at])
+        for index in range(5):
+            row, column = divmod(index, 4)
+            rows_ref[index : index + 1, pl.ds(block * WIDTH, WIDTH)] = sums[
+                row : row + 1, column * WIDTH : (column + 1) * WIDTH
+            ]
 
     received = received_ref[...]
     own = own_ref[...]
@@ -261,21 +307,26 @@
     for index, distance in enumerate((0, 3, 1, 2)):
         for at in (2 * index, 2 * index + 1):
             copy(sources[at][0], weights_ref.at[at], 8 + at).wait()
-        inner = dot(normed, weights_ref[2 * index]) + around_ref[distance, pl.ds(5, 1), :]
+        inner = dot(normed, weights_ref[2 * index]) + whole_rows(around_ref[distance])[2:3]
         active = jax.nn.gelu(inner, approximate=True).astype(jnp.bfloat16)
         total_ref[...] += dot(active, weights_ref[2 * index + 1])
     finished = norm_rows(total_ref[...], rows_ref[3:4, :], rows_ref[4:5, :]).astype(out_ref.dtype)
     for block in range(4):
         for u in range(2):
-            out_ref[pl.ds(block * 128, 128), pl.ds(u * WIDTH, WIDTH)] = finished[
+            folded_ref[pl.ds(block * 128, 128), pl.ds(u * WIDTH, WIDTH)] = finished[
                 u * 128 : (u + 1) * 128, block * WIDTH : (block + 1) * WIDTH
             ]
+    out_ref[...] = folded_ref[...].reshape(out_ref.shape)
 
 
 VMEM = pl.BlockSpec(memory_space=pltpu.VMEM)
 HBM = pl.BlockSpec(memory_space=pltpu.HBM)
 ANYWHERE = pl.BlockSpec(memory_space=pl.ANY)
-PARAMS = pltpu.CompilerParams(vmem_limit_bytes=40 * 2**20)
+EXTRA = 32
+
+
+def params(mebibytes):
+    return pltpu.CompilerParams(vmem_limit_bytes=mebibytes * 2**20)
 
 
 def array(shape, dtype=jnp.bfloat16):
@@ -311,6 +362,18 @@
 def shift_hid(value, step):
     pairs = [(hid, (hid + step) % HID_DEVICES) for hid in range(HID_DEVICES)]
     return lax.ppermute(value, "hid", pairs)
+
+
+def low_matrices(after):
+    table, _ = lax.optimization_barrier((jnp.asarray(LOW_TABLE), after))
+    return pl.pallas_call(
+        turn_kernel,
+        out_shape=array((2, R, 2 * R)),
+        in_specs=[VMEM],
+        out_specs=VMEM,
+        compiler_params=params(8),
+        cost_estimate=pl.CostEstimate(flops=10**10, bytes_accessed=2 * 10**7, transcendentals=0),
+    )(table)
 
 
 def shards(
@@ -326,33 +389,46 @@
 ):
     bf16 = jnp.bfloat16
     f32 = jnp.float32
-    core = lax.axis_index("seq") & 1
-
-    payload = jnp.where(core == 0, inner_weight, outer_weight)
+
+    payload = pl.pallas_call(
+        payload_kernel,
+        out_shape=array((D + EXTRA, D)),
+        in_specs=[HBM] * 2 + [VMEM] * 6,
+        out_specs=VMEM,
+        scratch_shapes=[pltpu.VMEM((8, D), f32), pltpu.SemaphoreType.DMA],
+        compiler_params=params(62),
+    )(
+        inner_weight,
+        outer_weight,
+        first_gain,
+        first_shift,
+        outer_bias,
+        second_gain,
+        second_shift,
+        inner_bias,
+    )
     ring_one = ring(payload, 1)
-    ring_three = ring(payload, -1)
 
     tokens_t, _ = lax.optimization_barrier((tokens.T, payload))
     sent = pl.pallas_call(
         scatter_kernel,
-        out_shape=array((2 * R, HALF)),
+        out_shape=array(CHUNKS),
         in_specs=[VMEM],
         out_specs=VMEM,
         scratch_shapes=[pltpu.VMEM((HALF, 2 * R), bf16)],
-        compiler_params=PARAMS,
+        compiler_params=params(8),
     )(tokens_t)
     taken = lax.all_to_all(sent, EVERY, 0, 0, tiled=True)
 
-    vectors = (first_gain, first_shift, outer_bias, second_gain, second_shift)
-    vectors, _ = lax.optimization_barrier(((*vectors, inner_bias), sent))
-    small = jnp.stack([jnp.pad(each, (0, D - each.shape[0])) for each in vectors])
-    small = jnp.concatenate([small, jnp.zeros((2, D), f32)])
-    around = [small, shift_hid(small, -1), shift_hid(small, 2), shift_hid(small, 1)]
-    taken, _ = lax.optimization_barrier((taken, around))
+    matrices = low_matrices(sent)
+    (ring_one, late), _ = lax.optimization_barrier(((ring_one, payload), matrices))
+    ring_two, ring_three = ring(ring_one, 1), ring(late, -1)
+    swap_one = swap_cores(ring_one)
+    taken, _ = lax.optimization_barrier((taken, matrices))
 
     local, sent = pl.pallas_call(
         high_kernel,
-        out_shape=(array((R, D)), array((2 * R, HALF))),
+        out_shape=(array((R, D)), array(CHUNKS)),
         in_specs=[VMEM] * 3,
         out_specs=(HBM, VMEM),
         scratch_shapes=[
@@ -360,23 +436,12 @@
             pltpu.VMEM((2 * R, 2 * R), bf16),
             pltpu.SemaphoreType.DMA,
         ],
-        compiler_params=PARAMS,
+        compiler_params=params(16),
     )(taken, jnp.asarray(FEATURE), jnp.asarray(HIGH_TABLE))
     taken = lax.all_to_all(sent, EVERY, 0, 0, tiled=True)
 
-    (ring_one, ring_three), _ = lax.optimization_barrier(((ring_one, ring_three), sent))
-    ring_two = ring(ring_one, 1)
-    swap_one, swap_three = swap_cores(ring_one), swap_cores(ring_three)
-    turns, _ = lax.optimization_barrier((jnp.asarray(LOW_TURN), sent))
-    matrices = pl.pallas_call(
-        turn_kernel,
-        out_shape=array((2, R, 2 * R)),
-        in_specs=[HBM, VMEM],
-        out_specs=VMEM,
-        scratch_shapes=[pltpu.VMEM((4, 2 * R), f32), pltpu.SemaphoreType.DMA],
-        compiler_params=PARAMS,
-    )(turns, jnp.asarray(LOW_TABLE))
-    taken, _ = lax.optimization_barrier((taken, matrices))
+    (ring_two, ring_three), _ = lax.optimization_barrier(((ring_two, ring_three), taken))
+    swap_two, swap_three = swap_cores(ring_two), swap_cores(ring_three)
 
     own, other = pl.pallas_call(
         low_kernel,
@@ -384,40 +449,39 @@
         in_specs=[VMEM] * 2,
         out_specs=(VMEM, VMEM),
         scratch_shapes=[pltpu.VMEM((2 * R, 2 * R), bf16)],
-        compiler_params=PARAMS,
+        compiler_params=params(8),
     )(taken, matrices)
-    ring_two_there, _ = lax.optimization_barrier((ring_two, taken))
-    swap_two = swap_cores(ring_two_there)
     received = swap_mirrored(other)
 
     def layer(*refs):
-        return layer_kernel(*refs[:4], refs[4:8], *refs[8:10], refs[10:13], refs[13:16], *refs[16:])
+        return layer_kernel(*refs[:7], refs[7:10], refs[10:13], *refs[13:])
 
     sent = pl.pallas_call(
         layer,
-        out_shape=array((2 * R, HALF)),
-        in_specs=[ANYWHERE] * 16,
+        out_shape=array(CHUNKS),
+        in_specs=[ANYWHERE] * 2 + [HBM] * 2 + [ANYWHERE] * 9,
         out_specs=VMEM,
         scratch_shapes=[
             pltpu.VMEM((R, HALF), f32),
             pltpu.VMEM((R, HALF), bf16),
             pltpu.VMEM((HALF, HALF), bf16),
             pltpu.VMEM((R, D), bf16),
-            pltpu.VMEM((4, 8, D), f32),
+            pltpu.VMEM((4, EXTRA, D), bf16),
             pltpu.VMEM((8, D, D), bf16),
             pltpu.VMEM((8, D), f32),
             pltpu.VMEM((R, D), f32),
+            pltpu.VMEM((2 * R, HALF), bf16),
             pltpu.SemaphoreType.DMA((16,)),
         ],
-        compiler_params=PARAMS,
+        compiler_params=params(52),
     )(
         own,
         received,
         jnp.asarray(MIRROR),
         local,
-        *around,
         inner_weight,
         outer_weight,
+        payload,
         ring_one,
         ring_two,
         ring_three,
@@ -432,7 +496,7 @@
         out_shape=array(tokens.shape[::-1]),
         in_specs=[VMEM],
         out_specs=VMEM,
-        compiler_params=PARAMS,
+        compiler_params=params(8),
     )(taken).T
 
 

time: 113 us -> 106 us (0.938)
  starting transfers between devices: 41.2 us -> 28.4 us
  Pallas kernels: 9.97 us -> 15.2 us
  waiting for transfers between devices: 28 us -> 32.9 us
  local copies, waits for them, and re-layouts: 6.82 us -> 2.37 us
  other arithmetic: 2.46 us -> 0 us
  blocking collectives: 24.2 us -> 26.4 us
    all_to_all x2, starting transfers between devices: 27.5 us -> 18.9 us  [shards(): taken = lax.all_to_all(sent, EVERY, 0, 0, tiled=True)]
    ppermute x3 -> x0, starting transfers between devices: 5.04 us -> none  [shift_hid(): return lax.ppermute(value, 'hid', pairs)]
    pallas_call x4 -> x5, Pallas kernels: 8.17 us -> 13.2 us  [the longest x1 6.35 us: shards(): pl.pallas_call(layer, out_shape=array(CHUNKS), in_specs=[ANYWHERE] * 2 +...]
    all_to_all x2, waiting for transfers between devices: 26.3 us -> 30 us  [shards(): taken = lax.all_to_all(sent, EVERY, 0, 0, tiled=True)]
    all_to_all x6 -> x0, local copies, waits for them, and re-layouts: 3.37 us -> none  [shards(): taken = lax.all_to_all(sent, EVERY, 0, 0, tiled=True)]
    select_n x1 -> x0, other arithmetic: 2.46 us -> none  [shards(): payload = jnp.where(core == 0, inner_weight, outer_weight)]
    all_to_all x1, blocking collectives: 24.2 us -> 26.4 us  [shards(): taken = lax.all_to_all(sent, EVERY, 0, 0, tiled=True)]
    unnamed x32 -> x14, local copies, waits for them, and re-layouts: 3.35 us -> 2.37 us
  transfers between devices with their start and end apart: 12 -> 9, of which waited for: 3 -> 4; matrix products, arithmetic and copies ran while one was open for 0% -> 0% of each run, Pallas kernels for 2% -> 4%
where the time goes in v2:
time: 106 us; the launch traced here: 105 us
  waiting for transfers between devices  32.9 us (31%)
  starting transfers between devices  28.4 us (27%)
  blocking collectives  26.4 us (25%)
  Pallas kernels  15.2 us (14%)
  local copies, waits for them, and re-layouts  2.37 us (2%)
    all_to_all x2, waiting for transfers between devices, shards(): taken = lax.all_to_all(sent, EVERY, 0, 0, tiled=True)  30 us
    all_to_all x1, blocking collectives, shards(): taken = lax.all_to_all(sent, EVERY, 0, 0, tiled=True)  26.4 us
    all_to_all x2, starting transfers between devices, shards(): taken = lax.all_to_all(sent, EVERY, 0, 0, tiled=True)  18.9 us
    pallas_call x1, Pallas kernels, shards(): pl.pallas_call(layer, out_shape=array(CHUNKS), in_specs=[ANYWHERE] * 2 +...  6.35 us
    ppermute x3, starting transfers between devices, ring(): return lax.ppermute(value, ('seq', 'hid'), pairs)  6.15 us
    pallas_call x1, Pallas kernels, shards(): pl.pallas_call(payload_kernel, out_shape=array((D + EXTRA, D)), in_specs=...  3.16 us
    ppermute x3, waiting for transfers between devices, swap_cores(): lax.ppermute(value, 'seq', [(seq, seq ^ 1) for seq in range(SEQ_DEVICES)])  2.83 us
    ppermute x3, starting transfers between devices, swap_cores(): lax.ppermute(value, 'seq', [(seq, seq ^ 1) for seq in range(SEQ_DEVICES)])  2.52 us
  transfers between devices with their start and end apart: 9, of which 4 were waited for; matrix products, arithmetic and copies ran while one was open for 0% of the time, Pallas kernels for 4%

profile of v2, /device:TPU:1, one launch (start us, length us, event | category | flops | bytes accessed | tf_op | source)
XLA Modules:
  0.0 105.3 jit_solution(3911969627547404312)
XLA Ops:
  0.0 0.0 copy-start.2
  0.0 3.2 %shard_map.127.refs_6_ = bf16[800,768]{1,0:T(8,128)(2,1)} custom-call(bf16[768,768]{1,0:T(8,128)(2,1)} %refs_4_.1, bf16[768,768]{1,0:T(8,128)(2,1)} %refs_5_.1, f32[192]{0:T(256)} %rest_0_.1, f32[192]{0:T(256)} %rest_1_.1, f32[192]{0:T(256)} %rest_2_.1, f32[192]{0:T(256)} %rest_3_.1, f32[192]{0:T(256)} %rest_4_.1, f32[768]{0:T(1024)} %rest_5_.1), custom_call_target="tpu_custom_call" | custom-call | tf_op jit(solution)/shard_map/pallas_call | solution.py:393
  3.2 3.4 %collective-permute-start.1 = (bf16[800,768]{1,0:T(8,128)(2,1)}, bf16[800,768]{1,0:T(8,128)(2,1)}, u32[]{:S(2)}, u32[]{:S(2)}) collective-permute-start(bf16[800,768]{1,0:T(8,128)(2,1)} %shard_map.127.refs_6_), channel_id=1, source_target_pairs={{0,1},{1,2},{2,3},{3,0},{4,7},{5,4},{6,5},{7,6},{8,9},{9,10},{10,1... | collective-permute-start | bytes 3686408 | tf_op jit(solution)/shard_map/ppermute | solution.py:346
  6.6 0.0 copy-done.2
  6.6 1.3 %shard_map.128 = bf16[256,2,384]{2,1,0:T(2,128)(2,1)} custom-call(bf16[192,1024]{1,0:T(8,128)(2,1)S(1)} %bitcast.2), custom_call_target="tpu_custom_call" | custom-call | tf_op jit(solution)/shard_map/pallas_call | solution.py:413
  7.8 13.5 %all-to-all-start = ((bf16[256,2,384]{2,1,0:T(2,128)(2,1)}), bf16[256,2,384]{2,1,0:T(2,128)(2,1)S(1)}, u32[]{:S(2)}, u32[]{:S(2)}) async-start(bf16[256,2,384]{2,1,0:T(2,128)(2,1)} %shard_map.128), calls=%async_computation | async-start | bytes 786432 | tf_op jit(solution)/shard_map/all_to_all | solution.py:421
  21.4 0.0 copy-start.4
  21.4 1.2 %copy-done.4 = f32[2,256,512]{2,1,0:T(8,128)S(1)} copy-done((f32[2,256,512]{2,1,0:T(8,128)S(1)}, f32[2,256,512]{2,1,0:T(8,128)}, u32[]{:S(2)}) %copy-start.4) | copy-done | bytes 1048600
  22.6 0.0 copy-start
  22.6 0.0 copy-start.1
  22.6 0.2 shard_map.129.matrix_ref
  22.8 0.0 collective-permute-done.1.refs_7_
  22.8 1.5 %collective-permute-start.3 = (bf16[800,768]{1,0:T(8,128)(2,1)}, bf16[800,768]{1,0:T(8,128)(2,1)}, u32[]{:S(2)}, u32[]{:S(2)}) collective-permute-start(bf16[800,768]{1,0:T(8,128)(2,1)} %shard_map.127.refs_6_), channel_id=1, source_target_pairs={{0,3},{1,0},{2,1},{3,2},{4,5},{5,6},{6,7},{7,4},{8,11},{9,8},{10,9... | collective-permute-start | bytes 3686408 | tf_op jit(solution)/shard_map/ppermute | solution.py:346
  24.3 1.3 %collective-permute-start.2 = (bf16[800,768]{1,0:T(8,128)(2,1)}, bf16[800,768]{1,0:T(8,128)(2,1)}, u32[]{:S(2)}, u32[]{:S(2)}) collective-permute-start(bf16[800,768]{1,0:T(8,128)(2,1)} %collective-permute-done.1.refs_7_), channel_id=1, source_target_pairs={{0,1},{1,2},{2,3},{3,0},{4,7},{5,4},{6,5},{7,6},{8,9},{9,10},{10,1... | collective-permute-start | bytes 3686408 | tf_op jit(solution)/shard_map/ppermute | solution.py:346
  25.6 14.1 %all-to-all-done.taken_ref = bf16[256,2,384]{2,1,0:T(2,128)(2,1)S(1)} async-done(((bf16[256,2,384]{2,1,0:T(2,128)(2,1)}), bf16[256,2,384]{2,1,0:T(2,128)(2,1)S(1)}, u32[]{:S(2)}, u32[]{:S(2)}) %all-to-all-start) | async-done | bytes 393248 | tf_op jit(solution)/shard_map/all_to_all | solution.py:421
  39.7 0.0 copy-done
  39.7 0.0 copy-done.1
  39.7 2.2 %shard_map.130 = (bf16[256,768]{1,0:T(8,128)(2,1)S(1)}, bf16[256,2,384]{2,1,0:T(2,128)(2,1)}) custom-call(bf16[256,2,384]{2,1,0:T(2,128)(2,1)S(1)} %all-to-all-done.taken_ref, bf16[768,768]{1,0:T(8,128)(2,1)S(1)} %copy-done, bf16[512,512]{1,0:T(8,128)(2,1)S(1)} %copy-done.1), custom_call_target="tpu_custom_call" | custom-call | tf_op jit(solution)/shard_map/pallas_call | solution.py:429
  41.9 0.0 copy-start.3
  41.9 5.3 %all-to-all-start.1 = ((bf16[256,2,384]{2,1,0:T(2,128)(2,1)}), bf16[256,2,384]{2,1,0:T(2,128)(2,1)S(1)}, u32[]{:S(2)}, u32[]{:S(2)}) async-start(bf16[256,2,384]{2,1,0:T(2,128)(2,1)} %get-tuple-element.19), calls=%async_computation.1 | async-start | bytes 786432 | tf_op jit(solution)/shard_map/all_to_all | solution.py:441
  47.2 2.0 %collective-permute-start.4 = (bf16[800,768]{1,0:T(8,128)(2,1)}, bf16[800,768]{1,0:T(8,128)(2,1)}, u32[]{:S(2)}, u32[]{:S(2)}) collective-permute-start(bf16[800,768]{1,0:T(8,128)(2,1)} %collective-permute-done.1.refs_7_), channel_id=1, source_target_pairs={{0,4},{4,0},{8,12},{12,8},{16,20},{20,16},{24,28},{28,24},{32,36},... | collective-permute-start | bytes 3686408 | tf_op jit(solution)/shard_map/ppermute | solution.py:350
  49.2 16.0 %all-to-all-done.1.taken_ref = bf16[256,2,384]{2,1,0:T(2,128)(2,1)S(1)} async-done(((bf16[256,2,384]{2,1,0:T(2,128)(2,1)}), bf16[256,2,384]{2,1,0:T(2,128)(2,1)S(1)}, u32[]{:S(2)}, u32[]{:S(2)}) %all-to-all-start.1) | async-done | bytes 393248 | tf_op jit(solution)/shard_map/all_to_all | solution.py:441
  65.2 0.0 collective-permute-done.3.refs_9_
  65.2 0.0 collective-permute-done.2.refs_8_
  65.2 0.0 collective-permute-start.5
  65.2 0.5 collective-permute-start.6
  65.7 0.7 shard_map.131
  66.4 0.9 collective-permute-start
  67.2 0.0 collective-permute-done.refs_1_
  67.2 0.0 collective-permute-done.4.refs_10_
  67.3 1.1 %collective-permute-done.5.refs_11_ = bf16[800,768]{1,0:T(8,128)(2,1)S(1)} collective-permute-done((bf16[800,768]{1,0:T(8,128)(2,1)}, bf16[800,768]{1,0:T(8,128)(2,1)S(1)}, u32[]{:S(2)}, u32[]{:S(2)}) %collective-permute-start.5) | collective-permute-done | bytes 1228832 | tf_op jit(solution)/shard_map/ppermute | solution.py:350
  68.3 0.0 copy-start.5
  68.3 1.8 %collective-permute-done.6.refs_12_ = bf16[800,768]{1,0:T(8,128)(2,1)S(1)} collective-permute-done((bf16[800,768]{1,0:T(8,128)(2,1)}, bf16[800,768]{1,0:T(8,128)(2,1)S(1)}, u32[]{:S(2)}, u32[]{:S(2)}) %collective-permute-start.6) | collective-permute-done | bytes 1228832 | tf_op jit(solution)/shard_map/ppermute | solution.py:350
  70.1 0.0 copy-start.6
  70.1 0.0 copy-done.5
  70.1 1.1 %copy-done.6 = bf16[800,768]{1,0:T(8,128)(2,1)} copy-done((bf16[800,768]{1,0:T(8,128)(2,1)}, bf16[800,768]{1,0:T(8,128)(2,1)S(1)}, u32[]{:S(2)}) %copy-start.6) | copy-done | bytes 1228824
  71.2 0.0 copy-done.3
  71.2 6.3 %shard_map.132 = bf16[256,2,384]{2,1,0:T(2,128)(2,1)S(1)} custom-call(f32[256,384]{1,0:T(8,128)S(1)} %get-tuple-element.20.refs_0_, bf16[256,384]{1,0:T(8,128)(2,1)S(1)} %collective-permute-done.refs_1_, bf16[384,384]{1,0:T(8,128)(2,1)S(1)} %copy-done.3, bf16[256,768]{1,0:T(8,128)(2,1)S(1)} %get-tuple-element.22.refs_3_, bf16[768,768]{1,0:T(8,128)(2,1)} %refs_4_.1, ...), custom_call_target="tpu_custom_call" | custom-call | tf_op jit(solution)/shard_map/pallas_call | solution.py:459
  77.6 26.4 %all_to_all.15.taken_ref = bf16[256,2,384]{2,1,0:T(2,128)(2,1)S(1)} all-to-all(bf16[256,2,384]{2,1,0:T(2,128)(2,1)S(1)} %shard_map.132), channel_id=1, replica_groups=mesh['seq'=64,'hid'=4] {'hid','seq'}, dimensions={0} | all-to-all | bytes 786432 | tf_op jit(solution)/shard_map/all_to_all | solution.py:492
  103.9 1.3 %shard_map.133 = bf16[192,1024]{1,0:T(8,128)(2,1)} custom-call(bf16[256,2,384]{2,1,0:T(2,128)(2,1)S(1)} %all_to_all.15.taken_ref), custom_call_target="tpu_custom_call" | custom-call | tf_op jit(solution)/shard_map/pallas_call | solution.py:494
Async XLA Ops:
  0.0 6.6 %copy-start.2 = (bf16[1024,192]{0,1:T(8,128)(2,1)S(1)}, bf16[1024,192]{0,1:T(8,128)(2,1)}, u32[]{:S(2)}) copy-start(bf16[1024,192]{0,1:T(8,128)(2,1)} %param.13) | copy-start | bytes 1179652
  3.2 19.7 %collective-permute-start.1 = (bf16[800,768]{1,0:T(8,128)(2,1)}, bf16[800,768]{1,0:T(8,128)(2,1)}, u32[]{:S(2)}, u32[]{:S(2)}) collective-permute-start(bf16[800,768]{1,0:T(8,128)(2,1)} %shard_map.127.refs_6_), channel_id=1, source_target_pairs={{0,1},{1,2},{2,3},{3,0},{4,7},{5,4},{6,5},{7,6},{8,9},{9,10},{10,1... | collective-permute-start | bytes 3686408 | tf_op jit(solution)/shard_map/ppermute | solution.py:346
  7.8 31.9 %all-to-all-start = ((bf16[256,2,384]{2,1,0:T(2,128)(2,1)}), bf16[256,2,384]{2,1,0:T(2,128)(2,1)S(1)}, u32[]{:S(2)}, u32[]{:S(2)}) async-start(bf16[256,2,384]{2,1,0:T(2,128)(2,1)} %shard_map.128), calls=%async_computation | async-start | bytes 786432 | tf_op jit(solution)/shard_map/all_to_all | solution.py:421
  21.4 1.2 %copy-start.4 = (f32[2,256,512]{2,1,0:T(8,128)S(1)}, f32[2,256,512]{2,1,0:T(8,128)}, u32[]{:S(2)}) copy-start(f32[2,256,512]{2,1,0:T(8,128)} %constant.8.clone.table_ref) | copy-start | bytes 3145732
  22.6 17.1 %copy-start = (bf16[768,768]{1,0:T(8,128)(2,1)S(1)}, bf16[768,768]{1,0:T(8,128)(2,1)}, u32[]{:S(2)}) copy-start(bf16[768,768]{1,0:T(8,128)(2,1)} %constant.9.clone.feature_ref) | copy-start | bytes 3538948
  22.6 17.1 %copy-start.1 = (bf16[512,512]{1,0:T(8,128)(2,1)S(1)}, bf16[512,512]{1,0:T(8,128)(2,1)}, u32[]{:S(2)}) copy-start(bf16[512,512]{1,0:T(8,128)(2,1)} %constant.10.clone.table_ref) | copy-start | bytes 1572868
  22.8 42.4 %collective-permute-start.3 = (bf16[800,768]{1,0:T(8,128)(2,1)}, bf16[800,768]{1,0:T(8,128)(2,1)}, u32[]{:S(2)}, u32[]{:S(2)}) collective-permute-start(bf16[800,768]{1,0:T(8,128)(2,1)} %shard_map.127.refs_6_), channel_id=1, source_target_pairs={{0,3},{1,0},{2,1},{3,2},{4,5},{5,6},{6,7},{7,4},{8,11},{9,8},{10,9... | collective-permute-start | bytes 3686408 | tf_op jit(solution)/shard_map/ppermute | solution.py:346
  24.3 40.9 %collective-permute-start.2 = (bf16[800,768]{1,0:T(8,128)(2,1)}, bf16[800,768]{1,0:T(8,128)(2,1)}, u32[]{:S(2)}, u32[]{:S(2)}) collective-permute-start(bf16[800,768]{1,0:T(8,128)(2,1)} %collective-permute-done.1.refs_7_), channel_id=1, source_target_pairs={{0,1},{1,2},{2,3},{3,0},{4,7},{5,4},{6,5},{7,6},{8,9},{9,10},{10,1... | collective-permute-start | bytes 3686408 | tf_op jit(solution)/shard_map/ppermute | solution.py:346
  41.9 29.3 %copy-start.3 = (bf16[384,384]{1,0:T(8,128)(2,1)S(1)}, bf16[384,384]{1,0:T(8,128)(2,1)}, u32[]{:S(2)}) copy-start(bf16[384,384]{1,0:T(8,128)(2,1)} %constant.11.clone.refs_2_) | copy-start | bytes 884740
  41.9 23.3 %all-to-all-start.1 = ((bf16[256,2,384]{2,1,0:T(2,128)(2,1)}), bf16[256,2,384]{2,1,0:T(2,128)(2,1)S(1)}, u32[]{:S(2)}, u32[]{:S(2)}) async-start(bf16[256,2,384]{2,1,0:T(2,128)(2,1)} %get-tuple-element.19), calls=%async_computation.1 | async-start | bytes 786432 | tf_op jit(solution)/shard_map/all_to_all | solution.py:441
  47.2 20.0 %collective-permute-start.4 = (bf16[800,768]{1,0:T(8,128)(2,1)}, bf16[800,768]{1,0:T(8,128)(2,1)}, u32[]{:S(2)}, u32[]{:S(2)}) collective-permute-start(bf16[800,768]{1,0:T(8,128)(2,1)} %collective-permute-done.1.refs_7_), channel_id=1, source_target_pairs={{0,4},{4,0},{8,12},{12,8},{16,20},{20,16},{24,28},{28,24},{32,36},... | collective-permute-start | bytes 3686408 | tf_op jit(solution)/shard_map/ppermute | solution.py:350
  65.2 3.1 %collective-permute-start.5 = (bf16[800,768]{1,0:T(8,128)(2,1)}, bf16[800,768]{1,0:T(8,128)(2,1)S(1)}, u32[]{:S(2)}, u32[]{:S(2)}) collective-permute-start(bf16[800,768]{1,0:T(8,128)(2,1)} %collective-permute-done.2.refs_8_), channel_id=1, source_target_pairs={{0,4},{4,0},{8,12},{12,8},{16,20},{20,16},{24,28},{28,24},{32,36},... | collective-permute-start | bytes 3686408 | tf_op jit(solution)/shard_map/ppermute | solution.py:350
  65.2 4.9 %collective-permute-start.6 = (bf16[800,768]{1,0:T(8,128)(2,1)}, bf16[800,768]{1,0:T(8,128)(2,1)S(1)}, u32[]{:S(2)}, u32[]{:S(2)}) collective-permute-start(bf16[800,768]{1,0:T(8,128)(2,1)} %collective-permute-done.3.refs_9_), channel_id=1, source_target_pairs={{0,4},{4,0},{8,12},{12,8},{16,20},{20,16},{24,28},{28,24},{32,36},... | collective-permute-start | bytes 3686408 | tf_op jit(solution)/shard_map/ppermute | solution.py:350
  66.4 0.9 collective-permute-start
  68.3 1.8 %copy-start.5 = (bf16[800,768]{1,0:T(8,128)(2,1)}, bf16[800,768]{1,0:T(8,128)(2,1)S(1)}, u32[]{:S(2)}) copy-start(bf16[800,768]{1,0:T(8,128)(2,1)S(1)} %collective-permute-done.5.refs_11_) | copy-start | bytes 3686404
  70.1 1.1 %copy-start.6 = (bf16[800,768]{1,0:T(8,128)(2,1)}, bf16[800,768]{1,0:T(8,128)(2,1)S(1)}, u32[]{:S(2)}) copy-start(bf16[800,768]{1,0:T(8,128)(2,1)S(1)} %collective-permute-done.6.refs_12_) | copy-start | bytes 3686404

commit v3 on v2

--- a/solution.py
+++ b/solution.py
@@ -1,3 +1,4 @@
+import functools
 import math
 
 import jax
@@ -181,7 +182,7 @@
     keep.wait()
 
 
-def turn_kernel(table_ref, out_ref):
+def turn_kernel(opposed, table_ref, out_ref):
     residue = residue_of(lax.axis_index("hid") * SEQ_DEVICES + lax.axis_index("seq"))
     column = lax.broadcasted_iota(jnp.int32, (8, 2 * R), 1)
     opposite = jnp.where(residue == 0, 0, R - residue)
@@ -190,12 +191,12 @@
     angle = phase.astype(jnp.float32) * (2.0 * math.pi / SEQ)
     sign = jnp.where(jnp.logical_or(row == 0, column % 2 == 0), 1.0, -1.0)
     cosine, sine = jnp.cos(angle) * sign, jnp.sin(angle) * sign
-    for index in range(2):
-        matrix = table_ref[0] * cosine[index : index + 1] + table_ref[1] * sine[index : index + 1]
-        out_ref[index] = matrix.astype(out_ref.dtype)
-
-
-def low_kernel(taken_ref, matrix_ref, own_ref, other_ref, wide_ref):
+    index = int(opposed)
+    matrix = table_ref[0] * cosine[index : index + 1] + table_ref[1] * sine[index : index + 1]
+    out_ref[...] = matrix.astype(out_ref.dtype)
+
+
+def low_kernel(taken_ref, first_ref, second_ref, own_ref, other_ref, wide_ref):
     scale = 1.0 / math.sqrt(SEQ * D)
     alone = jnp.logical_and(lax.axis_index("hid") == 0, lax.axis_index("seq") < 2)
     taken = taken_ref[...].reshape(2 * R, HALF)
@@ -208,8 +209,8 @@
     wide_ref[:, pl.ds(HALF, 128)] = edge.astype(wide_ref.dtype)
     lane = lax.broadcasted_iota(jnp.int32, (R, 128), 1)
     single = jnp.logical_and(lane == 0, alone)
-    for index, out_ref in enumerate((own_ref, other_ref)):
-        usual = dot(matrix_ref[index], wide_ref[...]) * scale
+    for index, (matrix_ref, out_ref) in enumerate(((first_ref, own_ref), (second_ref, other_ref))):
+        usual = dot(matrix_ref[...], wide_ref[...]) * scale
         edge = usual[:, HALF + index : HALF + index + 1]
         out_ref[:, pl.ds(0, 128)] = jnp.where(single, edge, usual[:, :128]).astype(out_ref.dtype)
         out_ref[:, pl.ds(128, HALF - 128)] = usual[:, 128:HALF].astype(out_ref.dtype)
@@ -304,10 +305,16 @@
     first_sum = local_ref[...].astype(jnp.float32) + mixed
     normed = norm_rows(first_sum, rows_ref[0:1, :], rows_ref[1:2, :]).astype(jnp.bfloat16)
     total_ref[...] = normed.astype(jnp.float32) + rows_ref[2:3, :]
-    for index, distance in enumerate((0, 3, 1, 2)):
+    def project(index):
         for at in (2 * index, 2 * index + 1):
             copy(sources[at][0], weights_ref.at[at], 8 + at).wait()
-        inner = dot(normed, weights_ref[2 * index]) + whole_rows(around_ref[distance])[2:3]
+        return dot(normed, weights_ref[2 * index])
+
+    later = project(0)
+    for index, distance in enumerate((0, 3, 1, 2)):
+        inner = later + whole_rows(around_ref[distance])[2:3]
+        if index < 3:
+            later = project(index + 1)
         active = jax.nn.gelu(inner, approximate=True).astype(jnp.bfloat16)
         total_ref[...] += dot(active, weights_ref[2 * index + 1])
     finished = norm_rows(total_ref[...], rows_ref[3:4, :], rows_ref[4:5, :]).astype(out_ref.dtype)
@@ -323,6 +330,7 @@
 HBM = pl.BlockSpec(memory_space=pltpu.HBM)
 ANYWHERE = pl.BlockSpec(memory_space=pl.ANY)
 EXTRA = 32
+HIDDEN = pl.CostEstimate(flops=10**10, bytes_accessed=2 * 10**7, transcendentals=0)
 
 
 def params(mebibytes):
@@ -364,15 +372,15 @@
     return lax.ppermute(value, "hid", pairs)
 
 
-def low_matrices(after):
+def low_matrix(opposed, after):
     table, _ = lax.optimization_barrier((jnp.asarray(LOW_TABLE), after))
     return pl.pallas_call(
-        turn_kernel,
-        out_shape=array((2, R, 2 * R)),
+        functools.partial(turn_kernel, opposed),
+        out_shape=array((R, 2 * R)),
         in_specs=[VMEM],
         out_specs=VMEM,
         compiler_params=params(8),
-        cost_estimate=pl.CostEstimate(flops=10**10, bytes_accessed=2 * 10**7, transcendentals=0),
+        cost_estimate=HIDDEN,
     )(table)
 
 
@@ -420,11 +428,11 @@
     )(tokens_t)
     taken = lax.all_to_all(sent, EVERY, 0, 0, tiled=True)
 
-    matrices = low_matrices(sent)
-    (ring_one, late), _ = lax.optimization_barrier(((ring_one, payload), matrices))
+    own_matrix = low_matrix(False, sent)
+    (ring_one, late), _ = lax.optimization_barrier(((ring_one, payload), own_matrix))
     ring_two, ring_three = ring(ring_one, 1), ring(late, -1)
     swap_one = swap_cores(ring_one)
-    taken, _ = lax.optimization_barrier((taken, matrices))
+    taken, _ = lax.optimization_barrier((taken, own_matrix))
 
     local, sent = pl.pallas_call(
         high_kernel,
@@ -440,17 +448,19 @@
     )(taken, jnp.asarray(FEATURE), jnp.asarray(HIGH_TABLE))
     taken = lax.all_to_all(sent, EVERY, 0, 0, tiled=True)
 
-    (ring_two, ring_three), _ = lax.optimization_barrier(((ring_two, ring_three), taken))
+    other_matrix = low_matrix(True, sent)
+    (ring_two, ring_three), _ = lax.optimization_barrier(((ring_two, ring_three), other_matrix))
     swap_two, swap_three = swap_cores(ring_two), swap_cores(ring_three)
 
     own, other = pl.pallas_call(
         low_kernel,
         out_shape=(array((R, HALF), f32), array((R, HALF))),
-        in_specs=[VMEM] * 2,
+        in_specs=[VMEM] * 3,
         out_specs=(VMEM, VMEM),
         scratch_shapes=[pltpu.VMEM((2 * R, 2 * R), bf16)],
         compiler_params=params(8),
-    )(taken, matrices)
+        cost_estimate=HIDDEN,
+    )(taken, own_matrix, other_matrix)
     received = swap_mirrored(other)
 
     def layer(*refs):

time: 106 us -> 104 us (0.981)
  waiting for transfers between devices: 32.9 us -> 28.5 us
  blocking collectives: 26.4 us -> 28.6 us
  local copies, waits for them, and re-layouts: 2.37 us -> 0.75 us
  starting transfers between devices: 28.4 us -> 29.8 us
    all_to_all x2, waiting for transfers between devices: 30 us -> 19.7 us  [shards(): taken = lax.all_to_all(sent, EVERY, 0, 0, tiled=True)]
    ppermute x3, waiting for transfers between devices: 0.01 us -> 8.84 us  [ring(): return lax.ppermute(value, ('seq', 'hid'), pairs)]
    ppermute x3, waiting for transfers between devices: 2.83 us -> 0.01 us  [swap_cores(): lax.ppermute(value, 'seq', [(seq, seq ^ 1) for seq in range(SEQ_DEVICES)])]
    all_to_all x1, blocking collectives: 26.4 us -> 28.6 us  [shards(): taken = lax.all_to_all(sent, EVERY, 0, 0, tiled=True)]
    unnamed x14, local copies, waits for them, and re-layouts: 2.37 us -> 0.75 us
    ppermute x3, starting transfers between devices: 2.52 us -> 4.11 us  [swap_cores(): lax.ppermute(value, 'seq', [(seq, seq ^ 1) for seq in range(SEQ_DEVICES)])]
where the time goes in v3:
time: 104 us; the launch traced here: 103 us
  starting transfers between devices  29.8 us (29%)
  blocking collectives  28.6 us (28%)
  waiting for transfers between devices  28.5 us (27%)
  Pallas kernels  15.5 us (15%)
    all_to_all x1, blocking collectives, shards(): taken = lax.all_to_all(sent, EVERY, 0, 0, tiled=True)  28.6 us
    all_to_all x2, waiting for transfers between devices, shards(): taken = lax.all_to_all(sent, EVERY, 0, 0, tiled=True)  19.7 us
    all_to_all x2, starting transfers between devices, shards(): taken = lax.all_to_all(sent, EVERY, 0, 0, tiled=True)  18.7 us
    ppermute x3, waiting for transfers between devices, ring(): return lax.ppermute(value, ('seq', 'hid'), pairs)  8.84 us
    pallas_call x1, Pallas kernels, shards(): pl.pallas_call(layer, out_shape=array(CHUNKS), in_specs=[ANYWHERE] * 2 +...  6.56 us
    ppermute x3, starting transfers between devices, ring(): return lax.ppermute(value, ('seq', 'hid'), pairs)  6.06 us
    ppermute x3, starting transfers between devices, swap_cores(): lax.ppermute(value, 'seq', [(seq, seq ^ 1) for seq in range(SEQ_DEVICES)])  4.11 us
    pallas_call x1, Pallas kernels, shards(): pl.pallas_call(payload_kernel, out_shape=array((D + EXTRA, D)), in_specs=...  3.16 us
  transfers between devices with their start and end apart: 9, of which 4 were waited for; matrix products, arithmetic and copies ran while one was open for 0% of the time, Pallas kernels for 4%

profile of v3, /device:TPU:1, one launch (start us, length us, event | category | flops | bytes accessed | tf_op | source)
XLA Modules:
  0.0 103.3 jit_solution(6608048560588091575)
XLA Ops:
  0.0 0.0 copy-start.2
  0.0 3.2 %shard_map.127.refs_6_ = bf16[800,768]{1,0:T(8,128)(2,1)} custom-call(bf16[768,768]{1,0:T(8,128)(2,1)} %refs_4_.1, bf16[768,768]{1,0:T(8,128)(2,1)} %refs_5_.1, f32[192]{0:T(256)} %rest_0_.1, f32[192]{0:T(256)} %rest_1_.1, f32[192]{0:T(256)} %rest_2_.1, f32[192]{0:T(256)} %rest_3_.1, f32[192]{0:T(256)} %rest_4_.1, f32[768]{0:T(1024)} %rest_5_.1), custom_call_target="tpu_custom_call" | custom-call | tf_op jit(solution)/shard_map/pallas_call | solution.py:401
  3.2 0.0 copy-start.4
  3.2 3.4 %collective-permute-start.1 = (bf16[800,768]{1,0:T(8,128)(2,1)}, bf16[800,768]{1,0:T(8,128)(2,1)}, u32[]{:S(2)}, u32[]{:S(2)}) collective-permute-start(bf16[800,768]{1,0:T(8,128)(2,1)} %shard_map.127.refs_6_), channel_id=1, source_target_pairs={{0,1},{1,2},{2,3},{3,0},{4,7},{5,4},{6,5},{7,6},{8,9},{9,10},{10,1... | collective-permute-start | bytes 3686408 | tf_op jit(solution)/shard_map/ppermute | solution.py:354
  6.6 0.0 copy-done.2
  6.6 1.3 %shard_map.128 = bf16[256,2,384]{2,1,0:T(2,128)(2,1)} custom-call(bf16[192,1024]{1,0:T(8,128)(2,1)S(1)} %bitcast.2), custom_call_target="tpu_custom_call" | custom-call | tf_op jit(solution)/shard_map/pallas_call | solution.py:421
  7.8 13.5 %all-to-all-start = ((bf16[256,2,384]{2,1,0:T(2,128)(2,1)}), bf16[256,2,384]{2,1,0:T(2,128)(2,1)S(1)}, u32[]{:S(2)}, u32[]{:S(2)}) async-start(bf16[256,2,384]{2,1,0:T(2,128)(2,1)} %shard_map.128), calls=%async_computation | async-start | bytes 786432 | tf_op jit(solution)/shard_map/all_to_all | solution.py:429
  21.4 0.0 copy-done.4
  21.4 0.0 copy-start
  21.4 0.0 copy-start.1
  21.4 0.2 shard_map.129.first_ref
  21.6 0.0 copy-start.5
  21.6 0.7 copy-done.5
  22.3 0.0 collective-permute-done.1.refs_7_
  22.3 1.4 %collective-permute-start.3 = (bf16[800,768]{1,0:T(8,128)(2,1)}, bf16[800,768]{1,0:T(8,128)(2,1)}, u32[]{:S(2)}, u32[]{:S(2)}) collective-permute-start(bf16[800,768]{1,0:T(8,128)(2,1)} %shard_map.127.refs_6_), channel_id=1, source_target_pairs={{0,3},{1,0},{2,1},{3,2},{4,5},{5,6},{6,7},{7,4},{8,11},{9,8},{10,9... | collective-permute-start | bytes 3686408 | tf_op jit(solution)/shard_map/ppermute | solution.py:354
  23.7 1.3 %collective-permute-start.2 = (bf16[800,768]{1,0:T(8,128)(2,1)}, bf16[800,768]{1,0:T(8,128)(2,1)}, u32[]{:S(2)}, u32[]{:S(2)}) collective-permute-start(bf16[800,768]{1,0:T(8,128)(2,1)} %collective-permute-done.1.refs_7_), channel_id=1, source_target_pairs={{0,1},{1,2},{2,3},{3,0},{4,7},{5,4},{6,5},{7,6},{8,9},{9,10},{10,1... | collective-permute-start | bytes 3686408 | tf_op jit(solution)/shard_map/ppermute | solution.py:354
  25.0 14.7 %all-to-all-done.taken_ref = bf16[256,2,384]{2,1,0:T(2,128)(2,1)S(1)} async-done(((bf16[256,2,384]{2,1,0:T(2,128)(2,1)}), bf16[256,2,384]{2,1,0:T(2,128)(2,1)S(1)}, u32[]{:S(2)}, u32[]{:S(2)}) %all-to-all-start) | async-done | bytes 393248 | tf_op jit(solution)/shard_map/all_to_all | solution.py:429
  39.7 0.0 copy-done
  39.7 0.0 copy-done.1
  39.7 2.2 %shard_map.130 = (bf16[256,768]{1,0:T(8,128)(2,1)S(1)}, bf16[256,2,384]{2,1,0:T(2,128)(2,1)}) custom-call(bf16[256,2,384]{2,1,0:T(2,128)(2,1)S(1)} %all-to-all-done.taken_ref, bf16[768,768]{1,0:T(8,128)(2,1)S(1)} %copy-done, bf16[512,512]{1,0:T(8,128)(2,1)S(1)} %copy-done.1), custom_call_target="tpu_custom_call" | custom-call | tf_op jit(solution)/shard_map/pallas_call | solution.py:437
  41.9 5.2 %all-to-all-start.1 = ((bf16[256,2,384]{2,1,0:T(2,128)(2,1)}), bf16[256,2,384]{2,1,0:T(2,128)(2,1)S(1)}, u32[]{:S(2)}, u32[]{:S(2)}) async-start(bf16[256,2,384]{2,1,0:T(2,128)(2,1)} %get-tuple-element.20), calls=%async_computation.1 | async-start | bytes 786432 | tf_op jit(solution)/shard_map/all_to_all | solution.py:449
  47.1 0.0 copy-start.6
  47.1 0.2 shard_map.131.second_ref
  47.3 0.0 copy-start.3
  47.3 2.1 %collective-permute-start.4 = (bf16[800,768]{1,0:T(8,128)(2,1)}, bf16[800,768]{1,0:T(8,128)(2,1)}, u32[]{:S(2)}, u32[]{:S(2)}) collective-permute-start(bf16[800,768]{1,0:T(8,128)(2,1)} %collective-permute-done.1.refs_7_), channel_id=1, source_target_pairs={{0,4},{4,0},{8,12},{12,8},{16,20},{20,16},{24,28},{28,24},{32,36},... | collective-permute-start | bytes 3686408 | tf_op jit(solution)/shard_map/ppermute | solution.py:358
  49.4 5.8 %collective-permute-done.3.refs_9_ = bf16[800,768]{1,0:T(8,128)(2,1)} collective-permute-done((bf16[800,768]{1,0:T(8,128)(2,1)}, bf16[800,768]{1,0:T(8,128)(2,1)}, u32[]{:S(2)}, u32[]{:S(2)}) %collective-permute-start.3) | collective-permute-done | bytes 1228832 | tf_op jit(solution)/shard_map/ppermute | solution.py:354
  55.2 3.1 %collective-permute-done.2.refs_8_ = bf16[800,768]{1,0:T(8,128)(2,1)} collective-permute-done((bf16[800,768]{1,0:T(8,128)(2,1)}, bf16[800,768]{1,0:T(8,128)(2,1)}, u32[]{:S(2)}, u32[]{:S(2)}) %collective-permute-start.2) | collective-permute-done | bytes 1228832 | tf_op jit(solution)/shard_map/ppermute | solution.py:354
  58.2 2.0 %collective-permute-start.5 = (bf16[800,768]{1,0:T(8,128)(2,1)}, bf16[800,768]{1,0:T(8,128)(2,1)}, u32[]{:S(2)}, u32[]{:S(2)}) collective-permute-start(bf16[800,768]{1,0:T(8,128)(2,1)} %collective-permute-done.2.refs_8_), channel_id=1, source_target_pairs={{0,4},{4,0},{8,12},{12,8},{16,20},{20,16},{24,28},{28,24},{32,36},... | collective-permute-start | bytes 3686408 | tf_op jit(solution)/shard_map/ppermute | solution.py:358
  60.2 0.0 collective-permute-start.6
  60.2 5.0 %all-to-all-done.1.taken_ref = bf16[256,2,384]{2,1,0:T(2,128)(2,1)S(1)} async-done(((bf16[256,2,384]{2,1,0:T(2,128)(2,1)}), bf16[256,2,384]{2,1,0:T(2,128)(2,1)S(1)}, u32[]{:S(2)}, u32[]{:S(2)}) %all-to-all-start.1) | async-done | bytes 393248 | tf_op jit(solution)/shard_map/all_to_all | solution.py:449
  65.2 0.0 copy-done.6
  65.2 0.7 shard_map.132
  65.9 0.9 collective-permute-start
  66.7 0.0 collective-permute-done.refs_1_
  66.7 0.0 collective-permute-done.4.refs_10_
  66.7 0.0 collective-permute-done.5.refs_11_
  66.7 0.0 collective-permute-done.6.refs_12_
  66.8 0.0 copy-done.3
  66.8 6.6 %shard_map.133 = bf16[256,2,384]{2,1,0:T(2,128)(2,1)S(1)} custom-call(f32[256,384]{1,0:T(8,128)S(1)} %get-tuple-element.22.refs_0_, bf16[256,384]{1,0:T(8,128)(2,1)S(1)} %collective-permute-done.refs_1_, bf16[384,384]{1,0:T(8,128)(2,1)S(1)} %copy-done.3, bf16[256,768]{1,0:T(8,128)(2,1)S(1)} %get-tuple-element.24.refs_3_, bf16[768,768]{1,0:T(8,128)(2,1)} %refs_4_.1, ...), custom_call_target="tpu_custom_call" | custom-call | tf_op jit(solution)/shard_map/pallas_call | solution.py:469
  73.3 28.6 %all_to_all.15.taken_ref = bf16[256,2,384]{2,1,0:T(2,128)(2,1)S(1)} all-to-all(bf16[256,2,384]{2,1,0:T(2,128)(2,1)S(1)} %shard_map.133), channel_id=1, replica_groups=mesh['seq'=64,'hid'=4] {'hid','seq'}, dimensions={0} | all-to-all | bytes 786432 | tf_op jit(solution)/shard_map/all_to_all | solution.py:502
  101.9 1.3 %shard_map.134 = bf16[192,1024]{1,0:T(8,128)(2,1)} custom-call(bf16[256,2,384]{2,1,0:T(2,128)(2,1)S(1)} %all_to_all.15.taken_ref), custom_call_target="tpu_custom_call" | custom-call | tf_op jit(solution)/shard_map/pallas_call | solution.py:504
Async XLA Ops:
  0.0 6.6 %copy-start.2 = (bf16[1024,192]{0,1:T(8,128)(2,1)S(1)}, bf16[1024,192]{0,1:T(8,128)(2,1)}, u32[]{:S(2)}) copy-start(bf16[1024,192]{0,1:T(8,128)(2,1)} %param.13) | copy-start | bytes 1179652
  3.2 18.2 %copy-start.4 = (f32[2,256,512]{2,1,0:T(8,128)S(1)}, f32[2,256,512]{2,1,0:T(8,128)}, u32[]{:S(2)}) copy-start(f32[2,256,512]{2,1,0:T(8,128)} %constant.8.clone.table_ref) | copy-start | bytes 3145732
  3.2 19.1 %collective-permute-start.1 = (bf16[800,768]{1,0:T(8,128)(2,1)}, bf16[800,768]{1,0:T(8,128)(2,1)}, u32[]{:S(2)}, u32[]{:S(2)}) collective-permute-start(bf16[800,768]{1,0:T(8,128)(2,1)} %shard_map.127.refs_6_), channel_id=1, source_target_pairs={{0,1},{1,2},{2,3},{3,0},{4,7},{5,4},{6,5},{7,6},{8,9},{9,10},{10,1... | collective-permute-start | bytes 3686408 | tf_op jit(solution)/shard_map/ppermute | solution.py:354
  7.8 31.9 %all-to-all-start = ((bf16[256,2,384]{2,1,0:T(2,128)(2,1)}), bf16[256,2,384]{2,1,0:T(2,128)(2,1)S(1)}, u32[]{:S(2)}, u32[]{:S(2)}) async-start(bf16[256,2,384]{2,1,0:T(2,128)(2,1)} %shard_map.128), calls=%async_computation | async-start | bytes 786432 | tf_op jit(solution)/shard_map/all_to_all | solution.py:429
  21.4 18.3 %copy-start = (bf16[768,768]{1,0:T(8,128)(2,1)S(1)}, bf16[768,768]{1,0:T(8,128)(2,1)}, u32[]{:S(2)}) copy-start(bf16[768,768]{1,0:T(8,128)(2,1)} %constant.9.clone.feature_ref) | copy-start | bytes 3538948
  21.4 18.3 %copy-start.1 = (bf16[512,512]{1,0:T(8,128)(2,1)S(1)}, bf16[512,512]{1,0:T(8,128)(2,1)}, u32[]{:S(2)}) copy-start(bf16[512,512]{1,0:T(8,128)(2,1)} %constant.10.clone.table_ref) | copy-start | bytes 1572868
  21.6 0.7 copy-start.5
  22.3 32.9 %collective-permute-start.3 = (bf16[800,768]{1,0:T(8,128)(2,1)}, bf16[800,768]{1,0:T(8,128)(2,1)}, u32[]{:S(2)}, u32[]{:S(2)}) collective-permute-start(bf16[800,768]{1,0:T(8,128)(2,1)} %shard_map.127.refs_6_), channel_id=1, source_target_pairs={{0,3},{1,0},{2,1},{3,2},{4,5},{5,6},{6,7},{7,4},{8,11},{9,8},{10,9... | collective-permute-start | bytes 3686408 | tf_op jit(solution)/shard_map/ppermute | solution.py:354
  23.7 34.6 %collective-permute-start.2 = (bf16[800,768]{1,0:T(8,128)(2,1)}, bf16[800,768]{1,0:T(8,128)(2,1)}, u32[]{:S(2)}, u32[]{:S(2)}) collective-permute-start(bf16[800,768]{1,0:T(8,128)(2,1)} %collective-permute-done.1.refs_7_), channel_id=1, source_target_pairs={{0,1},{1,2},{2,3},{3,0},{4,7},{5,4},{6,5},{7,6},{8,9},{9,10},{10,1... | collective-permute-start | bytes 3686408 | tf_op jit(solution)/shard_map/ppermute | solution.py:354
  41.9 23.3 %all-to-all-start.1 = ((bf16[256,2,384]{2,1,0:T(2,128)(2,1)}), bf16[256,2,384]{2,1,0:T(2,128)(2,1)S(1)}, u32[]{:S(2)}, u32[]{:S(2)}) async-start(bf16[256,2,384]{2,1,0:T(2,128)(2,1)} %get-tuple-element.20), calls=%async_computation.1 | async-start | bytes 786432 | tf_op jit(solution)/shard_map/all_to_all | solution.py:449
  47.1 18.1 %copy-start.6 = (bf16[256,512]{1,0:T(8,128)(2,1)S(1)}, bf16[256,512]{1,0:T(8,128)(2,1)}, u32[]{:S(2)}) copy-start(bf16[256,512]{1,0:T(8,128)(2,1)} %copy-done.5) | copy-start | bytes 786436
  47.3 19.5 %copy-start.3 = (bf16[384,384]{1,0:T(8,128)(2,1)S(1)}, bf16[384,384]{1,0:T(8,128)(2,1)}, u32[]{:S(2)}) copy-start(bf16[384,384]{1,0:T(8,128)(2,1)} %constant.11.clone.refs_2_) | copy-start | bytes 884740
  47.3 19.5 %collective-permute-start.4 = (bf16[800,768]{1,0:T(8,128)(2,1)}, bf16[800,768]{1,0:T(8,128)(2,1)}, u32[]{:S(2)}, u32[]{:S(2)}) collective-permute-start(bf16[800,768]{1,0:T(8,128)(2,1)} %collective-permute-done.1.refs_7_), channel_id=1, source_target_pairs={{0,4},{4,0},{8,12},{12,8},{16,20},{20,16},{24,28},{28,24},{32,36},... | collective-permute-start | bytes 3686408 | tf_op jit(solution)/shard_map/ppermute | solution.py:358
  58.2 8.5 %collective-permute-start.5 = (bf16[800,768]{1,0:T(8,128)(2,1)}, bf16[800,768]{1,0:T(8,128)(2,1)}, u32[]{:S(2)}, u32[]{:S(2)}) collective-permute-start(bf16[800,768]{1,0:T(8,128)(2,1)} %collective-permute-done.2.refs_8_), channel_id=1, source_target_pairs={{0,4},{4,0},{8,12},{12,8},{16,20},{20,16},{24,28},{28,24},{32,36},... | collective-permute-start | bytes 3686408 | tf_op jit(solution)/shard_map/ppermute | solution.py:358
  60.2 6.5 %collective-permute-start.6 = (bf16[800,768]{1,0:T(8,128)(2,1)}, bf16[800,768]{1,0:T(8,128)(2,1)}, u32[]{:S(2)}, u32[]{:S(2)}) collective-permute-start(bf16[800,768]{1,0:T(8,128)(2,1)} %collective-permute-done.3.refs_9_), channel_id=1, source_target_pairs={{0,4},{4,0},{8,12},{12,8},{16,20},{20,16},{24,28},{28,24},{32,36},... | collective-permute-start | bytes 3686408 | tf_op jit(solution)/shard_map/ppermute | solution.py:358
  65.9 0.9 collective-permute-start

commit v4 on v3

--- a/solution.py
+++ b/solution.py
@@ -99,18 +99,33 @@
 
 
 def payload_kernel(inner_ref, outer_ref, *rest):
-    *vector_refs, payload_ref, rows_ref, semaphore = rest
+    sources, rest = rest[:6], rest[6:]
+    payload_ref, held_ref, parts_ref, rows_ref, *vector_refs, semaphores = rest
+    vectors = [
+        pltpu.make_async_copy(source, target, semaphores.at[9 + at])
+        for at, (source, target) in enumerate(zip(sources, vector_refs))
+    ]
+    for each in vectors:
+        each.start()
     core = lax.rem(lax.axis_index("seq"), 2)
-    weights = payload_ref.at[pl.ds(0, D)]
+    pieces_of_rows = [pl.ds(at * WIDTH, WIDTH) for at in range(4)]
+
+    def fetch(source, at):
+        rows = pieces_of_rows[at]
+        return pltpu.make_async_copy(source.at[rows], held_ref.at[rows], semaphores.at[at])
 
     @pl.when(core == 0)
     def _():
-        pltpu.make_async_copy(inner_ref, weights, semaphore).start()
+        for at in range(4):
+            fetch(inner_ref, at).start()
 
     @pl.when(core == 1)
     def _():
-        pltpu.make_async_copy(outer_ref, weights, semaphore).start()
-
+        for at in range(4):
+            fetch(outer_ref, at).start()
+
+    for each in vectors:
+        each.wait()
     rows_ref[...] = jnp.zeros_like(rows_ref)
     for index, each in enumerate(vector_refs):
         row, at = divmod(index, 4) if index < 5 else (2, 0)
@@ -121,8 +136,17 @@
         pieces.append(rest.astype(jnp.bfloat16).astype(jnp.float32))
         rest = rest - pieces[-1]
     pieces.append(jnp.zeros_like(rest))
-    payload_ref[pl.ds(D, EXTRA), :] = jnp.concatenate(pieces, axis=0).astype(jnp.bfloat16)
-    pltpu.make_async_copy(inner_ref, weights, semaphore).wait()
+    parts_ref[...] = jnp.concatenate(pieces, axis=0).astype(jnp.bfloat16)
+    copies = [pltpu.make_async_copy(parts_ref, payload_ref.at[pl.ds(D, EXTRA)], semaphores.at[8])]
+    copies[0].start()
+    for at, rows in enumerate(pieces_of_rows):
+        fetch(inner_ref, at).wait()
+        copies.append(
+            pltpu.make_async_copy(held_ref.at[rows], payload_ref.at[rows], semaphores.at[4 + at])
+        )
+        copies[-1].start()
+    for each in copies:
+        each.wait()
 
 
 def scatter_kernel(tokens_ref, out_ref, wide_ref):
@@ -401,9 +425,16 @@
     payload = pl.pallas_call(
         payload_kernel,
         out_shape=array((D + EXTRA, D)),
-        in_specs=[HBM] * 2 + [VMEM] * 6,
-        out_specs=VMEM,
-        scratch_shapes=[pltpu.VMEM((8, D), f32), pltpu.SemaphoreType.DMA],
+        in_specs=[HBM] * 8,
+        out_specs=HBM,
+        scratch_shapes=[
+            pltpu.VMEM((D, D), bf16),
+            pltpu.VMEM((EXTRA, D), bf16),
+            pltpu.VMEM((8, D), f32),
+            *[pltpu.VMEM((WIDTH,), f32)] * 5,
+            pltpu.VMEM((D,), f32),
+            pltpu.SemaphoreType.DMA((15,)),
+        ],
         compiler_params=params(62),
     )(
         inner_weight,

time: 104 us -> 103 us (level)
  no operation moved by 1% of the time
where the time goes in v4:
time: 103 us; the launch traced here: 102 us
  starting transfers between devices  29.8 us (29%)
  blocking collectives  28.6 us (28%)
  waiting for transfers between devices  28.5 us (28%)
  Pallas kernels  14.6 us (14%)
    all_to_all x1, blocking collectives, shards(): taken = lax.all_to_all(sent, EVERY, 0, 0, tiled=True)  28.6 us
    all_to_all x2, waiting for transfers between devices, shards(): taken = lax.all_to_all(sent, EVERY, 0, 0, tiled=True)  19.7 us
    all_to_all x2, starting transfers between devices, shards(): taken = lax.all_to_all(sent, EVERY, 0, 0, tiled=True)  18.7 us
    ppermute x3, waiting for transfers between devices, ring(): return lax.ppermute(value, ('seq', 'hid'), pairs)  8.84 us
    pallas_call x1, Pallas kernels, shards(): pl.pallas_call(layer, out_shape=array(CHUNKS), in_specs=[ANYWHERE] * 2 +...  6.56 us
    ppermute x3, starting transfers between devices, ring(): return lax.ppermute(value, ('seq', 'hid'), pairs)  6.06 us
    ppermute x3, starting transfers between devices, swap_cores(): lax.ppermute(value, 'seq', [(seq, seq ^ 1) for seq in range(SEQ_DEVICES)])  4.12 us
    pallas_call x1, Pallas kernels, shards(): pl.pallas_call(payload_kernel, out_shape=array((D + EXTRA, D)), in_specs=...  2.29 us
  transfers between devices with their start and end apart: 9, of which 4 were waited for; matrix products, arithmetic and copies ran while one was open for 0% of the time, Pallas kernels for 4%

profile of v4, /device:TPU:1, one launch (start us, length us, event | category | flops | bytes accessed | tf_op | source)
XLA Modules:
  0.0 102.4 jit_solution(9682481228823526224)
XLA Ops:
  0.0 0.0 copy-start.2
  0.0 2.3 %shard_map.127.refs_6_ = bf16[800,768]{1,0:T(8,128)(2,1)} custom-call(bf16[768,768]{1,0:T(8,128)(2,1)} %refs_4_.1, bf16[768,768]{1,0:T(8,128)(2,1)} %refs_5_.1, f32[192]{0:T(256)} %rest_0_.1, f32[192]{0:T(256)} %rest_1_.1, f32[192]{0:T(256)} %rest_2_.1, f32[192]{0:T(256)} %rest_3_.1, f32[192]{0:T(256)} %rest_4_.1, f32[768]{0:T(1024)} %rest_5_.1), custom_call_target="tpu_custom_call" | custom-call | tf_op jit(solution)/shard_map/pallas_call | solution.py:425
  2.3 0.0 copy-start.4
  2.3 3.4 %collective-permute-start.1 = (bf16[800,768]{1,0:T(8,128)(2,1)}, bf16[800,768]{1,0:T(8,128)(2,1)}, u32[]{:S(2)}, u32[]{:S(2)}) collective-permute-start(bf16[800,768]{1,0:T(8,128)(2,1)} %shard_map.127.refs_6_), channel_id=1, source_target_pairs={{0,1},{1,2},{2,3},{3,0},{4,7},{5,4},{6,5},{7,6},{8,9},{9,10},{10,1... | collective-permute-start | bytes 3686408 | tf_op jit(solution)/shard_map/ppermute | solution.py:378
  5.7 0.0 copy-done.2
  5.7 1.3 %shard_map.128 = bf16[256,2,384]{2,1,0:T(2,128)(2,1)} custom-call(bf16[192,1024]{1,0:T(8,128)(2,1)S(1)} %bitcast.2), custom_call_target="tpu_custom_call" | custom-call | tf_op jit(solution)/shard_map/pallas_call | solution.py:452
  7.0 13.5 %all-to-all-start = ((bf16[256,2,384]{2,1,0:T(2,128)(2,1)}), bf16[256,2,384]{2,1,0:T(2,128)(2,1)S(1)}, u32[]{:S(2)}, u32[]{:S(2)}) async-start(bf16[256,2,384]{2,1,0:T(2,128)(2,1)} %shard_map.128), calls=%async_computation | async-start | bytes 786432 | tf_op jit(solution)/shard_map/all_to_all | solution.py:460
  20.5 0.0 copy-done.4
  20.5 0.0 copy-start
  20.5 0.0 copy-start.1
  20.5 0.2 shard_map.129.first_ref
  20.7 0.0 copy-start.5
  20.7 0.7 copy-done.5
  21.4 0.0 collective-permute-done.1.refs_7_
  21.4 1.4 %collective-permute-start.3 = (bf16[800,768]{1,0:T(8,128)(2,1)}, bf16[800,768]{1,0:T(8,128)(2,1)}, u32[]{:S(2)}, u32[]{:S(2)}) collective-permute-start(bf16[800,768]{1,0:T(8,128)(2,1)} %shard_map.127.refs_6_), channel_id=1, source_target_pairs={{0,3},{1,0},{2,1},{3,2},{4,5},{5,6},{6,7},{7,4},{8,11},{9,8},{10,9... | collective-permute-start | bytes 3686408 | tf_op jit(solution)/shard_map/ppermute | solution.py:378
  22.8 1.3 %collective-permute-start.2 = (bf16[800,768]{1,0:T(8,128)(2,1)}, bf16[800,768]{1,0:T(8,128)(2,1)}, u32[]{:S(2)}, u32[]{:S(2)}) collective-permute-start(bf16[800,768]{1,0:T(8,128)(2,1)} %collective-permute-done.1.refs_7_), channel_id=1, source_target_pairs={{0,1},{1,2},{2,3},{3,0},{4,7},{5,4},{6,5},{7,6},{8,9},{9,10},{10,1... | collective-permute-start | bytes 3686408 | tf_op jit(solution)/shard_map/ppermute | solution.py:378
  24.1 14.7 %all-to-all-done.taken_ref = bf16[256,2,384]{2,1,0:T(2,128)(2,1)S(1)} async-done(((bf16[256,2,384]{2,1,0:T(2,128)(2,1)}), bf16[256,2,384]{2,1,0:T(2,128)(2,1)S(1)}, u32[]{:S(2)}, u32[]{:S(2)}) %all-to-all-start) | async-done | bytes 393248 | tf_op jit(solution)/shard_map/all_to_all | solution.py:460
  38.8 0.0 copy-done
  38.8 0.0 copy-done.1
  38.8 2.2 %shard_map.130 = (bf16[256,768]{1,0:T(8,128)(2,1)S(1)}, bf16[256,2,384]{2,1,0:T(2,128)(2,1)}) custom-call(bf16[256,2,384]{2,1,0:T(2,128)(2,1)S(1)} %all-to-all-done.taken_ref, bf16[768,768]{1,0:T(8,128)(2,1)S(1)} %copy-done, bf16[512,512]{1,0:T(8,128)(2,1)S(1)} %copy-done.1), custom_call_target="tpu_custom_call" | custom-call | tf_op jit(solution)/shard_map/pallas_call | solution.py:468
  41.0 5.2 %all-to-all-start.1 = ((bf16[256,2,384]{2,1,0:T(2,128)(2,1)}), bf16[256,2,384]{2,1,0:T(2,128)(2,1)S(1)}, u32[]{:S(2)}, u32[]{:S(2)}) async-start(bf16[256,2,384]{2,1,0:T(2,128)(2,1)} %get-tuple-element.20), calls=%async_computation.1 | async-start | bytes 786432 | tf_op jit(solution)/shard_map/all_to_all | solution.py:480
  46.2 0.0 copy-start.6
  46.2 0.2 shard_map.131.second_ref
  46.4 0.0 copy-start.3
  46.4 2.1 %collective-permute-start.4 = (bf16[800,768]{1,0:T(8,128)(2,1)}, bf16[800,768]{1,0:T(8,128)(2,1)}, u32[]{:S(2)}, u32[]{:S(2)}) collective-permute-start(bf16[800,768]{1,0:T(8,128)(2,1)} %collective-permute-done.1.refs_7_), channel_id=1, source_target_pairs={{0,4},{4,0},{8,12},{12,8},{16,20},{20,16},{24,28},{28,24},{32,36},... | collective-permute-start | bytes 3686408 | tf_op jit(solution)/shard_map/ppermute | solution.py:382
  48.5 5.8 %collective-permute-done.3.refs_9_ = bf16[800,768]{1,0:T(8,128)(2,1)} collective-permute-done((bf16[800,768]{1,0:T(8,128)(2,1)}, bf16[800,768]{1,0:T(8,128)(2,1)}, u32[]{:S(2)}, u32[]{:S(2)}) %collective-permute-start.3) | collective-permute-done | bytes 1228832 | tf_op jit(solution)/shard_map/ppermute | solution.py:378
  54.3 3.1 %collective-permute-done.2.refs_8_ = bf16[800,768]{1,0:T(8,128)(2,1)} collective-permute-done((bf16[800,768]{1,0:T(8,128)(2,1)}, bf16[800,768]{1,0:T(8,128)(2,1)}, u32[]{:S(2)}, u32[]{:S(2)}) %collective-permute-start.2) | collective-permute-done | bytes 1228832 | tf_op jit(solution)/shard_map/ppermute | solution.py:378
  57.4 2.0 %collective-permute-start.5 = (bf16[800,768]{1,0:T(8,128)(2,1)}, bf16[800,768]{1,0:T(8,128)(2,1)}, u32[]{:S(2)}, u32[]{:S(2)}) collective-permute-start(bf16[800,768]{1,0:T(8,128)(2,1)} %collective-permute-done.2.refs_8_), channel_id=1, source_target_pairs={{0,4},{4,0},{8,12},{12,8},{16,20},{20,16},{24,28},{28,24},{32,36},... | collective-permute-start | bytes 3686408 | tf_op jit(solution)/shard_map/ppermute | solution.py:382
  59.4 0.0 collective-permute-start.6
  59.4 5.0 %all-to-all-done.1.taken_ref = bf16[256,2,384]{2,1,0:T(2,128)(2,1)S(1)} async-done(((bf16[256,2,384]{2,1,0:T(2,128)(2,1)}), bf16[256,2,384]{2,1,0:T(2,128)(2,1)S(1)}, u32[]{:S(2)}, u32[]{:S(2)}) %all-to-all-start.1) | async-done | bytes 393248 | tf_op jit(solution)/shard_map/all_to_all | solution.py:480
  64.3 0.0 copy-done.6
  64.3 0.7 shard_map.132
  65.0 0.9 collective-permute-start
  65.8 0.0 collective-permute-done.refs_1_
  65.9 0.0 collective-permute-done.4.refs_10_
  65.9 0.0 collective-permute-done.5.refs_11_
  65.9 0.0 collective-permute-done.6.refs_12_
  65.9 0.0 copy-done.3
  65.9 6.6 %shard_map.133 = bf16[256,2,384]{2,1,0:T(2,128)(2,1)S(1)} custom-call(f32[256,384]{1,0:T(8,128)S(1)} %get-tuple-element.22.refs_0_, bf16[256,384]{1,0:T(8,128)(2,1)S(1)} %collective-permute-done.refs_1_, bf16[384,384]{1,0:T(8,128)(2,1)S(1)} %copy-done.3, bf16[256,768]{1,0:T(8,128)(2,1)S(1)} %get-tuple-element.24.refs_3_, bf16[768,768]{1,0:T(8,128)(2,1)} %refs_4_.1, ...), custom_call_target="tpu_custom_call" | custom-call | tf_op jit(solution)/shard_map/pallas_call | solution.py:500
  72.5 28.6 %all_to_all.15.taken_ref = bf16[256,2,384]{2,1,0:T(2,128)(2,1)S(1)} all-to-all(bf16[256,2,384]{2,1,0:T(2,128)(2,1)S(1)} %shard_map.133), channel_id=1, replica_groups=mesh['seq'=64,'hid'=4] {'hid','seq'}, dimensions={0} | all-to-all | bytes 786432 | tf_op jit(solution)/shard_map/all_to_all | solution.py:533
  101.1 1.3 %shard_map.134 = bf16[192,1024]{1,0:T(8,128)(2,1)} custom-call(bf16[256,2,384]{2,1,0:T(2,128)(2,1)S(1)} %all_to_all.15.taken_ref), custom_call_target="tpu_custom_call" | custom-call | tf_op jit(solution)/shard_map/pallas_call | solution.py:535
Async XLA Ops:
  0.0 5.7 %copy-start.2 = (bf16[1024,192]{0,1:T(8,128)(2,1)S(1)}, bf16[1024,192]{0,1:T(8,128)(2,1)}, u32[]{:S(2)}) copy-start(bf16[1024,192]{0,1:T(8,128)(2,1)} %param.13) | copy-start | bytes 1179652
  2.3 18.2 %copy-start.4 = (f32[2,256,512]{2,1,0:T(8,128)S(1)}, f32[2,256,512]{2,1,0:T(8,128)}, u32[]{:S(2)}) copy-start(f32[2,256,512]{2,1,0:T(8,128)} %constant.8.clone.table_ref) | copy-start | bytes 3145732
  2.3 19.1 %collective-permute-start.1 = (bf16[800,768]{1,0:T(8,128)(2,1)}, bf16[800,768]{1,0:T(8,128)(2,1)}, u32[]{:S(2)}, u32[]{:S(2)}) collective-permute-start(bf16[800,768]{1,0:T(8,128)(2,1)} %shard_map.127.refs_6_), channel_id=1, source_target_pairs={{0,1},{1,2},{2,3},{3,0},{4,7},{5,4},{6,5},{7,6},{8,9},{9,10},{10,1... | collective-permute-start | bytes 3686408 | tf_op jit(solution)/shard_map/ppermute | solution.py:378
  7.0 31.9 %all-to-all-start = ((bf16[256,2,384]{2,1,0:T(2,128)(2,1)}), bf16[256,2,384]{2,1,0:T(2,128)(2,1)S(1)}, u32[]{:S(2)}, u32[]{:S(2)}) async-start(bf16[256,2,384]{2,1,0:T(2,128)(2,1)} %shard_map.128), calls=%async_computation | async-start | bytes 786432 | tf_op jit(solution)/shard_map/all_to_all | solution.py:460
  20.5 18.3 %copy-start = (bf16[768,768]{1,0:T(8,128)(2,1)S(1)}, bf16[768,768]{1,0:T(8,128)(2,1)}, u32[]{:S(2)}) copy-start(bf16[768,768]{1,0:T(8,128)(2,1)} %constant.9.clone.feature_ref) | copy-start | bytes 3538948
  20.5 18.3 %copy-start.1 = (bf16[512,512]{1,0:T(8,128)(2,1)S(1)}, bf16[512,512]{1,0:T(8,128)(2,1)}, u32[]{:S(2)}) copy-start(bf16[512,512]{1,0:T(8,128)(2,1)} %constant.10.clone.table_ref) | copy-start | bytes 1572868
  20.7 0.7 copy-start.5
  21.4 32.9 %collective-permute-start.3 = (bf16[800,768]{1,0:T(8,128)(2,1)}, bf16[800,768]{1,0:T(8,128)(2,1)}, u32[]{:S(2)}, u32[]{:S(2)}) collective-permute-start(bf16[800,768]{1,0:T(8,128)(2,1)} %shard_map.127.refs_6_), channel_id=1, source_target_pairs={{0,3},{1,0},{2,1},{3,2},{4,5},{5,6},{6,7},{7,4},{8,11},{9,8},{10,9... | collective-permute-start | bytes 3686408 | tf_op jit(solution)/shard_map/ppermute | solution.py:378
  22.8 34.6 %collective-permute-start.2 = (bf16[800,768]{1,0:T(8,128)(2,1)}, bf16[800,768]{1,0:T(8,128)(2,1)}, u32[]{:S(2)}, u32[]{:S(2)}) collective-permute-start(bf16[800,768]{1,0:T(8,128)(2,1)} %collective-permute-done.1.refs_7_), channel_id=1, source_target_pairs={{0,1},{1,2},{2,3},{3,0},{4,7},{5,4},{6,5},{7,6},{8,9},{9,10},{10,1... | collective-permute-start | bytes 3686408 | tf_op jit(solution)/shard_map/ppermute | solution.py:378
  41.0 23.3 %all-to-all-start.1 = ((bf16[256,2,384]{2,1,0:T(2,128)(2,1)}), bf16[256,2,384]{2,1,0:T(2,128)(2,1)S(1)}, u32[]{:S(2)}, u32[]{:S(2)}) async-start(bf16[256,2,384]{2,1,0:T(2,128)(2,1)} %get-tuple-element.20), calls=%async_computation.1 | async-start | bytes 786432 | tf_op jit(solution)/shard_map/all_to_all | solution.py:480
  46.2 18.1 %copy-start.6 = (bf16[256,512]{1,0:T(8,128)(2,1)S(1)}, bf16[256,512]{1,0:T(8,128)(2,1)}, u32[]{:S(2)}) copy-start(bf16[256,512]{1,0:T(8,128)(2,1)} %copy-done.5) | copy-start | bytes 786436
  46.4 19.5 %copy-start.3 = (bf16[384,384]{1,0:T(8,128)(2,1)S(1)}, bf16[384,384]{1,0:T(8,128)(2,1)}, u32[]{:S(2)}) copy-start(bf16[384,384]{1,0:T(8,128)(2,1)} %constant.11.clone.refs_2_) | copy-start | bytes 884740
  46.4 19.5 %collective-permute-start.4 = (bf16[800,768]{1,0:T(8,128)(2,1)}, bf16[800,768]{1,0:T(8,128)(2,1)}, u32[]{:S(2)}, u32[]{:S(2)}) collective-permute-start(bf16[800,768]{1,0:T(8,128)(2,1)} %collective-permute-done.1.refs_7_), channel_id=1, source_target_pairs={{0,4},{4,0},{8,12},{12,8},{16,20},{20,16},{24,28},{28,24},{32,36},... | collective-permute-start | bytes 3686408 | tf_op jit(solution)/shard_map/ppermute | solution.py:382
  57.4 8.5 %collective-permute-start.5 = (bf16[800,768]{1,0:T(8,128)(2,1)}, bf16[800,768]{1,0:T(8,128)(2,1)}, u32[]{:S(2)}, u32[]{:S(2)}) collective-permute-start(bf16[800,768]{1,0:T(8,128)(2,1)} %collective-permute-done.2.refs_8_), channel_id=1, source_target_pairs={{0,4},{4,0},{8,12},{12,8},{16,20},{20,16},{24,28},{28,24},{32,36},... | collective-permute-start | bytes 3686408 | tf_op jit(solution)/shard_map/ppermute | solution.py:382
  59.4 6.5 %collective-permute-start.6 = (bf16[800,768]{1,0:T(8,128)(2,1)}, bf16[800,768]{1,0:T(8,128)(2,1)}, u32[]{:S(2)}, u32[]{:S(2)}) collective-permute-start(bf16[800,768]{1,0:T(8,128)(2,1)} %collective-permute-done.3.refs_9_), channel_id=1, source_target_pairs={{0,4},{4,0},{8,12},{12,8},{16,20},{20,16},{24,28},{28,24},{32,36},... | collective-permute-start | bytes 3686408 | tf_op jit(solution)/shard_map/ppermute | solution.py:382
  65.0 0.9 collective-permute-start

commit v5 on v4

--- a/solution.py
+++ b/solution.py
@@ -264,6 +264,7 @@
     weights_ref,
     rows_ref,
     total_ref,
+    active_ref,
     folded_ref,
     semaphores,
 ):
@@ -292,7 +293,7 @@
         outer_from.append(
             tuple(each.at[pl.ds(0, D)] for each in (swapped_refs[j], ring_refs[j]))
         )
-    sources = [each for pair in zip(inner_from, outer_from) for each in pair]
+    sources = inner_from + outer_from
 
     def small_copy(which, taken_by):
         source = small_from[which][taken_by].at[pl.ds(D, EXTRA)]
@@ -330,17 +331,20 @@
     normed = norm_rows(first_sum, rows_ref[0:1, :], rows_ref[1:2, :]).astype(jnp.bfloat16)
     total_ref[...] = normed.astype(jnp.float32) + rows_ref[2:3, :]
     def project(index):
-        for at in (2 * index, 2 * index + 1):
-            copy(sources[at][0], weights_ref.at[at], 8 + at).wait()
-        return dot(normed, weights_ref[2 * index])
+        copy(sources[index][0], weights_ref.at[index], 8 + index).wait()
+        return dot(normed, weights_ref[index])
 
     later = project(0)
     for index, distance in enumerate((0, 3, 1, 2)):
         inner = later + whole_rows(around_ref[distance])[2:3]
         if index < 3:
             later = project(index + 1)
-        active = jax.nn.gelu(inner, approximate=True).astype(jnp.bfloat16)
-        total_ref[...] += dot(active, weights_ref[2 * index + 1])
+        active_ref[:, pl.ds(index * D, D)] = jax.nn.gelu(inner, approximate=True).astype(
+            jnp.bfloat16
+        )
+    for at in range(4, 8):
+        copy(sources[at][0], weights_ref.at[at], 8 + at).wait()
+    total_ref[...] += dot(active_ref[...], weights_ref[4:8].reshape(4 * D, D))
     finished = norm_rows(total_ref[...], rows_ref[3:4, :], rows_ref[4:5, :]).astype(out_ref.dtype)
     for block in range(4):
         for u in range(2):
@@ -511,6 +515,7 @@
             pltpu.VMEM((8, D, D), bf16),
             pltpu.VMEM((8, D), f32),
             pltpu.VMEM((R, D), f32),
+            pltpu.VMEM((R, 4 * D), bf16),
             pltpu.VMEM((2 * R, HALF), bf16),
             pltpu.SemaphoreType.DMA((16,)),
         ],

time: 103 us -> 104 us (level)
  no operation moved by 1% of the time
where the time goes in v5:
time: 104 us; the launch traced here: 103 us
  starting transfers between devices  29.8 us (29%)
  blocking collectives  28.6 us (28%)
  waiting for transfers between devices  28.5 us (27%)
  Pallas kernels  15.5 us (15%)
    all_to_all x1, blocking collectives, shards(): taken = lax.all_to_all(sent, EVERY, 0, 0, tiled=True)  28.6 us
    all_to_all x2, waiting for transfers between devices, shards(): taken = lax.all_to_all(sent, EVERY, 0, 0, tiled=True)  19.7 us
    all_to_all x2, starting transfers between devices, shards(): taken = lax.all_to_all(sent, EVERY, 0, 0, tiled=True)  18.7 us
    ppermute x3, waiting for transfers between devices, ring(): return lax.ppermute(value, ('seq', 'hid'), pairs)  8.84 us
    pallas_call x1, Pallas kernels, shards(): pl.pallas_call(layer, out_shape=array(CHUNKS), in_specs=[ANYWHERE] * 2 +...  7.45 us
    ppermute x3, starting transfers between devices, ring(): return lax.ppermute(value, ('seq', 'hid'), pairs)  6.06 us
    ppermute x3, starting transfers between devices, swap_cores(): lax.ppermute(value, 'seq', [(seq, seq ^ 1) for seq in range(SEQ_DEVICES)])  4.12 us
    pallas_call x1, Pallas kernels, shards(): pl.pallas_call(payload_kernel, out_shape=array((D + EXTRA, D)), in_specs=...  2.29 us
  transfers between devices with their start and end apart: 9, of which 4 were waited for; matrix products, arithmetic and copies ran while one was open for 0% of the time, Pallas kernels for 4%

profile of v5, /device:TPU:1, one launch (start us, length us, event | category | flops | bytes accessed | tf_op | source)
XLA Modules:
  0.0 103.3 jit_solution(9477472202464608916)
XLA Ops:
  0.0 0.0 copy-start.2
  0.0 2.3 %shard_map.127.refs_6_ = bf16[800,768]{1,0:T(8,128)(2,1)} custom-call(bf16[768,768]{1,0:T(8,128)(2,1)} %refs_4_.1, bf16[768,768]{1,0:T(8,128)(2,1)} %refs_5_.1, f32[192]{0:T(256)} %rest_0_.1, f32[192]{0:T(256)} %rest_1_.1, f32[192]{0:T(256)} %rest_2_.1, f32[192]{0:T(256)} %rest_3_.1, f32[192]{0:T(256)} %rest_4_.1, f32[768]{0:T(1024)} %rest_5_.1), custom_call_target="tpu_custom_call" | custom-call | tf_op jit(solution)/shard_map/pallas_call | solution.py:429
  2.3 0.0 copy-start.4
  2.3 3.4 %collective-permute-start.1 = (bf16[800,768]{1,0:T(8,128)(2,1)}, bf16[800,768]{1,0:T(8,128)(2,1)}, u32[]{:S(2)}, u32[]{:S(2)}) collective-permute-start(bf16[800,768]{1,0:T(8,128)(2,1)} %shard_map.127.refs_6_), channel_id=1, source_target_pairs={{0,1},{1,2},{2,3},{3,0},{4,7},{5,4},{6,5},{7,6},{8,9},{9,10},{10,1... | collective-permute-start | bytes 3686408 | tf_op jit(solution)/shard_map/ppermute | solution.py:382
  5.7 0.0 copy-done.2
  5.7 1.3 %shard_map.128 = bf16[256,2,384]{2,1,0:T(2,128)(2,1)} custom-call(bf16[192,1024]{1,0:T(8,128)(2,1)S(1)} %bitcast.2), custom_call_target="tpu_custom_call" | custom-call | tf_op jit(solution)/shard_map/pallas_call | solution.py:456
  7.0 13.5 %all-to-all-start = ((bf16[256,2,384]{2,1,0:T(2,128)(2,1)}), bf16[256,2,384]{2,1,0:T(2,128)(2,1)S(1)}, u32[]{:S(2)}, u32[]{:S(2)}) async-start(bf16[256,2,384]{2,1,0:T(2,128)(2,1)} %shard_map.128), calls=%async_computation | async-start | bytes 786432 | tf_op jit(solution)/shard_map/all_to_all | solution.py:464
  20.5 0.0 copy-done.4
  20.5 0.0 copy-start
  20.5 0.0 copy-start.1
  20.5 0.2 shard_map.129.first_ref
  20.7 0.0 copy-start.5
  20.7 0.7 copy-done.5
  21.4 0.0 collective-permute-done.1.refs_7_
  21.4 1.4 %collective-permute-start.3 = (bf16[800,768]{1,0:T(8,128)(2,1)}, bf16[800,768]{1,0:T(8,128)(2,1)}, u32[]{:S(2)}, u32[]{:S(2)}) collective-permute-start(bf16[800,768]{1,0:T(8,128)(2,1)} %shard_map.127.refs_6_), channel_id=1, source_target_pairs={{0,3},{1,0},{2,1},{3,2},{4,5},{5,6},{6,7},{7,4},{8,11},{9,8},{10,9... | collective-permute-start | bytes 3686408 | tf_op jit(solution)/shard_map/ppermute | solution.py:382
  22.8 1.3 %collective-permute-start.2 = (bf16[800,768]{1,0:T(8,128)(2,1)}, bf16[800,768]{1,0:T(8,128)(2,1)}, u32[]{:S(2)}, u32[]{:S(2)}) collective-permute-start(bf16[800,768]{1,0:T(8,128)(2,1)} %collective-permute-done.1.refs_7_), channel_id=1, source_target_pairs={{0,1},{1,2},{2,3},{3,0},{4,7},{5,4},{6,5},{7,6},{8,9},{9,10},{10,1... | collective-permute-start | bytes 3686408 | tf_op jit(solution)/shard_map/ppermute | solution.py:382
  24.1 14.7 %all-to-all-done.taken_ref = bf16[256,2,384]{2,1,0:T(2,128)(2,1)S(1)} async-done(((bf16[256,2,384]{2,1,0:T(2,128)(2,1)}), bf16[256,2,384]{2,1,0:T(2,128)(2,1)S(1)}, u32[]{:S(2)}, u32[]{:S(2)}) %all-to-all-start) | async-done | bytes 393248 | tf_op jit(solution)/shard_map/all_to_all | solution.py:464
  38.8 0.0 copy-done
  38.8 0.0 copy-done.1
  38.8 2.2 %shard_map.130 = (bf16[256,768]{1,0:T(8,128)(2,1)S(1)}, bf16[256,2,384]{2,1,0:T(2,128)(2,1)}) custom-call(bf16[256,2,384]{2,1,0:T(2,128)(2,1)S(1)} %all-to-all-done.taken_ref, bf16[768,768]{1,0:T(8,128)(2,1)S(1)} %copy-done, bf16[512,512]{1,0:T(8,128)(2,1)S(1)} %copy-done.1), custom_call_target="tpu_custom_call" | custom-call | tf_op jit(solution)/shard_map/pallas_call | solution.py:472
  41.0 5.2 %all-to-all-start.1 = ((bf16[256,2,384]{2,1,0:T(2,128)(2,1)}), bf16[256,2,384]{2,1,0:T(2,128)(2,1)S(1)}, u32[]{:S(2)}, u32[]{:S(2)}) async-start(bf16[256,2,384]{2,1,0:T(2,128)(2,1)} %get-tuple-element.20), calls=%async_computation.1 | async-start | bytes 786432 | tf_op jit(solution)/shard_map/all_to_all | solution.py:484
  46.2 0.0 copy-start.6
  46.2 0.2 shard_map.131.second_ref
  46.4 0.0 copy-start.3
  46.4 2.1 %collective-permute-start.4 = (bf16[800,768]{1,0:T(8,128)(2,1)}, bf16[800,768]{1,0:T(8,128)(2,1)}, u32[]{:S(2)}, u32[]{:S(2)}) collective-permute-start(bf16[800,768]{1,0:T(8,128)(2,1)} %collective-permute-done.1.refs_7_), channel_id=1, source_target_pairs={{0,4},{4,0},{8,12},{12,8},{16,20},{20,16},{24,28},{28,24},{32,36},... | collective-permute-start | bytes 3686408 | tf_op jit(solution)/shard_map/ppermute | solution.py:386
  48.5 5.8 %collective-permute-done.3.refs_9_ = bf16[800,768]{1,0:T(8,128)(2,1)} collective-permute-done((bf16[800,768]{1,0:T(8,128)(2,1)}, bf16[800,768]{1,0:T(8,128)(2,1)}, u32[]{:S(2)}, u32[]{:S(2)}) %collective-permute-start.3) | collective-permute-done | bytes 1228832 | tf_op jit(solution)/shard_map/ppermute | solution.py:382
  54.3 3.1 %collective-permute-done.2.refs_8_ = bf16[800,768]{1,0:T(8,128)(2,1)} collective-permute-done((bf16[800,768]{1,0:T(8,128)(2,1)}, bf16[800,768]{1,0:T(8,128)(2,1)}, u32[]{:S(2)}, u32[]{:S(2)}) %collective-permute-start.2) | collective-permute-done | bytes 1228832 | tf_op jit(solution)/shard_map/ppermute | solution.py:382
  57.4 2.0 %collective-permute-start.5 = (bf16[800,768]{1,0:T(8,128)(2,1)}, bf16[800,768]{1,0:T(8,128)(2,1)}, u32[]{:S(2)}, u32[]{:S(2)}) collective-permute-start(bf16[800,768]{1,0:T(8,128)(2,1)} %collective-permute-done.2.refs_8_), channel_id=1, source_target_pairs={{0,4},{4,0},{8,12},{12,8},{16,20},{20,16},{24,28},{28,24},{32,36},... | collective-permute-start | bytes 3686408 | tf_op jit(solution)/shard_map/ppermute | solution.py:386
  59.4 0.0 collective-permute-start.6
  59.4 5.0 %all-to-all-done.1.taken_ref = bf16[256,2,384]{2,1,0:T(2,128)(2,1)S(1)} async-done(((bf16[256,2,384]{2,1,0:T(2,128)(2,1)}), bf16[256,2,384]{2,1,0:T(2,128)(2,1)S(1)}, u32[]{:S(2)}, u32[]{:S(2)}) %all-to-all-start.1) | async-done | bytes 393248 | tf_op jit(solution)/shard_map/all_to_all | solution.py:484
  64.3 0.0 copy-done.6
  64.3 0.7 shard_map.132
  65.0 0.9 collective-permute-start
  65.8 0.0 collective-permute-done.refs_1_
  65.9 0.0 collective-permute-done.4.refs_10_
  65.9 0.0 collective-permute-done.5.refs_11_
  65.9 0.0 collective-permute-done.6.refs_12_
  65.9 0.0 copy-done.3
  65.9 7.5 %shard_map.133 = bf16[256,2,384]{2,1,0:T(2,128)(2,1)S(1)} custom-call(f32[256,384]{1,0:T(8,128)S(1)} %get-tuple-element.22.refs_0_, bf16[256,384]{1,0:T(8,128)(2,1)S(1)} %collective-permute-done.refs_1_, bf16[384,384]{1,0:T(8,128)(2,1)S(1)} %copy-done.3, bf16[256,768]{1,0:T(8,128)(2,1)S(1)} %get-tuple-element.24.refs_3_, bf16[768,768]{1,0:T(8,128)(2,1)} %refs_4_.1, ...), custom_call_target="tpu_custom_call" | custom-call | tf_op jit(solution)/shard_map/pallas_call | solution.py:504
  73.4 28.6 %all_to_all.15.taken_ref = bf16[256,2,384]{2,1,0:T(2,128)(2,1)S(1)} all-to-all(bf16[256,2,384]{2,1,0:T(2,128)(2,1)S(1)} %shard_map.133), channel_id=1, replica_groups=mesh['seq'=64,'hid'=4] {'hid','seq'}, dimensions={0} | all-to-all | bytes 786432 | tf_op jit(solution)/shard_map/all_to_all | solution.py:538
  102.0 1.3 %shard_map.134 = bf16[192,1024]{1,0:T(8,128)(2,1)} custom-call(bf16[256,2,384]{2,1,0:T(2,128)(2,1)S(1)} %all_to_all.15.taken_ref), custom_call_target="tpu_custom_call" | custom-call | tf_op jit(solution)/shard_map/pallas_call | solution.py:540
Async XLA Ops:
  0.0 5.7 %copy-start.2 = (bf16[1024,192]{0,1:T(8,128)(2,1)S(1)}, bf16[1024,192]{0,1:T(8,128)(2,1)}, u32[]{:S(2)}) copy-start(bf16[1024,192]{0,1:T(8,128)(2,1)} %param.13) | copy-start | bytes 1179652
  2.3 18.2 %copy-start.4 = (f32[2,256,512]{2,1,0:T(8,128)S(1)}, f32[2,256,512]{2,1,0:T(8,128)}, u32[]{:S(2)}) copy-start(f32[2,256,512]{2,1,0:T(8,128)} %constant.8.clone.table_ref) | copy-start | bytes 3145732
  2.3 19.1 %collective-permute-start.1 = (bf16[800,768]{1,0:T(8,128)(2,1)}, bf16[800,768]{1,0:T(8,128)(2,1)}, u32[]{:S(2)}, u32[]{:S(2)}) collective-permute-start(bf16[800,768]{1,0:T(8,128)(2,1)} %shard_map.127.refs_6_), channel_id=1, source_target_pairs={{0,1},{1,2},{2,3},{3,0},{4,7},{5,4},{6,5},{7,6},{8,9},{9,10},{10,1... | collective-permute-start | bytes 3686408 | tf_op jit(solution)/shard_map/ppermute | solution.py:382
  7.0 31.9 %all-to-all-start = ((bf16[256,2,384]{2,1,0:T(2,128)(2,1)}), bf16[256,2,384]{2,1,0:T(2,128)(2,1)S(1)}, u32[]{:S(2)}, u32[]{:S(2)}) async-start(bf16[256,2,384]{2,1,0:T(2,128)(2,1)} %shard_map.128), calls=%async_computation | async-start | bytes 786432 | tf_op jit(solution)/shard_map/all_to_all | solution.py:464
  20.5 18.3 %copy-start = (bf16[768,768]{1,0:T(8,128)(2,1)S(1)}, bf16[768,768]{1,0:T(8,128)(2,1)}, u32[]{:S(2)}) copy-start(bf16[768,768]{1,0:T(8,128)(2,1)} %constant.9.clone.feature_ref) | copy-start | bytes 3538948
  20.5 18.3 %copy-start.1 = (bf16[512,512]{1,0:T(8,128)(2,1)S(1)}, bf16[512,512]{1,0:T(8,128)(2,1)}, u32[]{:S(2)}) copy-start(bf16[512,512]{1,0:T(8,128)(2,1)} %constant.10.clone.table_ref) | copy-start | bytes 1572868
  20.7 0.7 copy-start.5
  21.4 32.9 %collective-permute-start.3 = (bf16[800,768]{1,0:T(8,128)(2,1)}, bf16[800,768]{1,0:T(8,128)(2,1)}, u32[]{:S(2)}, u32[]{:S(2)}) collective-permute-start(bf16[800,768]{1,0:T(8,128)(2,1)} %shard_map.127.refs_6_), channel_id=1, source_target_pairs={{0,3},{1,0},{2,1},{3,2},{4,5},{5,6},{6,7},{7,4},{8,11},{9,8},{10,9... | collective-permute-start | bytes 3686408 | tf_op jit(solution)/shard_map/ppermute | solution.py:382
  22.8 34.6 %collective-permute-start.2 = (bf16[800,768]{1,0:T(8,128)(2,1)}, bf16[800,768]{1,0:T(8,128)(2,1)}, u32[]{:S(2)}, u32[]{:S(2)}) collective-permute-start(bf16[800,768]{1,0:T(8,128)(2,1)} %collective-permute-done.1.refs_7_), channel_id=1, source_target_pairs={{0,1},{1,2},{2,3},{3,0},{4,7},{5,4},{6,5},{7,6},{8,9},{9,10},{10,1... | collective-permute-start | bytes 3686408 | tf_op jit(solution)/shard_map/ppermute | solution.py:382
  41.0 23.3 %all-to-all-start.1 = ((bf16[256,2,384]{2,1,0:T(2,128)(2,1)}), bf16[256,2,384]{2,1,0:T(2,128)(2,1)S(1)}, u32[]{:S(2)}, u32[]{:S(2)}) async-start(bf16[256,2,384]{2,1,0:T(2,128)(2,1)} %get-tuple-element.20), calls=%async_computation.1 | async-start | bytes 786432 | tf_op jit(solution)/shard_map/all_to_all | solution.py:484
  46.2 18.1 %copy-start.6 = (bf16[256,512]{1,0:T(8,128)(2,1)S(1)}, bf16[256,512]{1,0:T(8,128)(2,1)}, u32[]{:S(2)}) copy-start(bf16[256,512]{1,0:T(8,128)(2,1)} %copy-done.5) | copy-start | bytes 786436
  46.4 19.5 %copy-start.3 = (bf16[384,384]{1,0:T(8,128)(2,1)S(1)}, bf16[384,384]{1,0:T(8,128)(2,1)}, u32[]{:S(2)}) copy-start(bf16[384,384]{1,0:T(8,128)(2,1)} %constant.11.clone.refs_2_) | copy-start | bytes 884740
  46.4 19.5 %collective-permute-start.4 = (bf16[800,768]{1,0:T(8,128)(2,1)}, bf16[800,768]{1,0:T(8,128)(2,1)}, u32[]{:S(2)}, u32[]{:S(2)}) collective-permute-start(bf16[800,768]{1,0:T(8,128)(2,1)} %collective-permute-done.1.refs_7_), channel_id=1, source_target_pairs={{0,4},{4,0},{8,12},{12,8},{16,20},{20,16},{24,28},{28,24},{32,36},... | collective-permute-start | bytes 3686408 | tf_op jit(solution)/shard_map/ppermute | solution.py:386
  57.4 8.5 %collective-permute-start.5 = (bf16[800,768]{1,0:T(8,128)(2,1)}, bf16[800,768]{1,0:T(8,128)(2,1)}, u32[]{:S(2)}, u32[]{:S(2)}) collective-permute-start(bf16[800,768]{1,0:T(8,128)(2,1)} %collective-permute-done.2.refs_8_), channel_id=1, source_target_pairs={{0,4},{4,0},{8,12},{12,8},{16,20},{20,16},{24,28},{28,24},{32,36},... | collective-permute-start | bytes 3686408 | tf_op jit(solution)/shard_map/ppermute | solution.py:386
  59.4 6.5 %collective-permute-start.6 = (bf16[800,768]{1,0:T(8,128)(2,1)}, bf16[800,768]{1,0:T(8,128)(2,1)}, u32[]{:S(2)}, u32[]{:S(2)}) collective-permute-start(bf16[800,768]{1,0:T(8,128)(2,1)} %collective-permute-done.3.refs_9_), channel_id=1, source_target_pairs={{0,4},{4,0},{8,12},{12,8},{16,20},{20,16},{24,28},{28,24},{32,36},... | collective-permute-start | bytes 3686408 | tf_op jit(solution)/shard_map/ppermute | solution.py:386
  65.0 0.9 collective-permute-start
